TPU v7x, 256 devices: a whole 4x4x8 slice. The times are simulated.
256 devices in a mesh: ctx: 64 (over x, z, core), head: 4 (over y).
Axes of the slice: x: 4, y: 4, z: 8, core: 2. Of those that a mesh axis runs over, the one named last changes fastest.
Arguments:
- queries: bfloat16 [8192, 1536], P('ctx', 'head'), may hold values from -16 to 16
- key_rows: bfloat16 [8192, 1536], P('ctx', 'head'), may hold values from -6 to 6
- value_rows: bfloat16 [8192, 1536], P('ctx', 'head'), may hold values from -6 to 6
- out_weight: bfloat16 [3072, 1536], P(None, 'head'), may hold values from -0.15625 to 0.15625
- grad_projected: bfloat16 [8192, 3072], P('ctx', 'head'), may hold values from -16 to 16
- segment_len: int32 [8], replicated, may hold values from 1 to 2048, 8192 in all
- block_order: int32 [128], replicated, may hold values from 0 to 127, each once
Outputs:
- projected: bfloat16 [8192, 3072], P('ctx', 'head')
- grad_queries: bfloat16 [8192, 1536], P('ctx', 'head')
- grad_keys: bfloat16 [8192, 1536], P('ctx', 'head')
- grad_values: bfloat16 [8192, 1536], P('ctx', 'head')
- grad_out_weight: float32 [3072, 1536], P('ctx', 'head')
Inputs may be any that keep to these rules, and one draw needn't show every extreme that they name: `segment_len`: the lengths sum to 8192; the longest is exactly 2048. `block_order`: each block index appears once.
All inputs are finite; a program needn't handle non-finite values.
Results may differ from a plain program's by a relative error of at most 0.04.
Values may be sent and summed in bfloat16 or wider, within the bound.
A program may use at most 128 MiB of HBM per device.

v0:
```python
import math

import jax
import jax.numpy as jnp
from jax import lax
from jax.sharding import PartitionSpec as P

HD = 128


NEG_FILL = -1e30


def segment_ids(first_row, length, half_rows, block_order, seg_ends):
    row_ids = first_row + jnp.arange(length, dtype=jnp.int32)
    block_ids = row_ids // half_rows
    table_ids = jnp.arange(block_order.shape[0], dtype=jnp.int32)
    placed = jnp.sum(
        jnp.where(block_ids[:, None] == table_ids[None, :], block_order[None, :], 0), axis=1
    )
    position = placed * half_rows + row_ids % half_rows
    return jnp.sum((position[:, None] >= seg_ends[None, :]).astype(jnp.int32), axis=1)


def split_tiles(array_in, length):
    tile_len = 512
    return array_in.reshape((length // tile_len, tile_len) + array_in.shape[1:])


def per_device(queries, key_rows, value_rows, out_weight, grad_projected, segment_len, block_order):
    tok_rows, width = queries.shape
    heads = width // HD
    scaling = 1.0 / math.sqrt(HD)
    half_rows = tok_rows // 2
    seg_ends = jnp.cumsum(segment_len)
    my_first = lax.axis_index("ctx") * tok_rows
    my_segments = segment_ids(my_first, tok_rows, half_rows, block_order, seg_ends)
    upstream = lax.all_gather(grad_projected, "head", axis=1, tiled=True)
    grad_attn = jnp.dot(upstream, out_weight, preferred_element_type=jnp.float32).astype(
        jnp.bfloat16
    )
    query_heads = queries.reshape(tok_rows, heads, HD)
    key_heads = key_rows.reshape(tok_rows, heads, HD)
    value_heads = value_rows.reshape(tok_rows, heads, HD)
    dout_heads = grad_attn.reshape(tok_rows, heads, HD)

    def key_tile(running, tile_in):
        maxima, totals, acc_out, acc_mix, acc_key = running
        key_t, value_t, segment_t = tile_in
        visible = segment_t[None, None, :] <= my_segments[None, :, None]
        scores = (
            jnp.einsum("qhd,khd->hqk", query_heads, key_t, preferred_element_type=jnp.float32)
            * scaling
        )
        scores = jnp.where(visible, scores, NEG_FILL)
        new_max = jnp.maximum(maxima, jnp.max(scores, axis=2))
        rescale = jnp.exp(maxima - new_max)
        weights = jnp.where(visible, jnp.exp(scores - new_max[:, :, None]), 0.0)
        totals = totals * rescale + jnp.sum(weights, axis=2)
        weights_low = weights.astype(jnp.bfloat16)
        acc_out = acc_out * rescale[:, :, None] + jnp.einsum(
            "hqk,khd->hqd", weights_low, value_t, preferred_element_type=jnp.float32
        )
        grad_prob = jnp.einsum(
            "qhd,khd->hqk", dout_heads, value_t, preferred_element_type=jnp.float32
        )
        acc_mix = acc_mix * rescale[:, :, None] + jnp.einsum(
            "hqk,khd->hqd",
            (weights * grad_prob).astype(jnp.bfloat16),
            key_t,
            preferred_element_type=jnp.float32,
        )
        acc_key = acc_key * rescale[:, :, None] + jnp.einsum(
            "hqk,khd->hqd", weights_low, key_t, preferred_element_type=jnp.float32
        )
        return (new_max, totals, acc_out, acc_mix, acc_key)

    def key_step(running, tile_in):
        return (key_tile(running, tile_in), None)

    zeros_acc = jnp.zeros((heads, tok_rows, HD), jnp.float32)
    start_state = (
        jnp.full((heads, tok_rows), NEG_FILL, jnp.float32),
        jnp.zeros((heads, tok_rows), jnp.float32),
        zeros_acc,
        zeros_acc,
        zeros_acc,
    )
    running = start_state
    key_piece = lax.all_gather(key_rows, "ctx", axis=0, tiled=True)
    value_piece = lax.all_gather(value_rows, "ctx", axis=0, tiled=True)
    length = key_piece.shape[0]
    segment_piece = segment_ids(jnp.int32(0), length, half_rows, block_order, seg_ends)
    tiles = (
        split_tiles(key_piece.reshape(length, heads, HD), length),
        split_tiles(value_piece.reshape(length, heads, HD), length),
        split_tiles(segment_piece, length),
    )
    running, unused = lax.scan(key_step, running, tiles)
    maxima, totals, acc_out, acc_mix, acc_key = running
    inverse = 1.0 / totals
    out_heads = acc_out * inverse[:, :, None]
    row_lse = maxima + jnp.log(totals)
    row_delta = jnp.sum(
        jnp.transpose(dout_heads, (1, 0, 2)).astype(jnp.float32) * out_heads, axis=2
    )
    grad_query = scaling * (acc_mix - row_delta[:, :, None] * acc_key) * inverse[:, :, None]

    def to_rows(array_in):
        return jnp.transpose(array_in, (1, 0, 2)).reshape(tok_rows, width)

    attended = to_rows(out_heads).astype(jnp.bfloat16)
    partial_proj = lax.dot_general(
        attended, out_weight, (((1,), (1,)), ((), ())), preferred_element_type=jnp.float32
    )
    projected = lax.psum_scatter(
        partial_proj.astype(jnp.bfloat16), "head", scatter_dimension=1, tiled=True
    )
    grad_weight = lax.psum_scatter(
        lax.dot_general(
            upstream, attended, (((0,), (0,)), ((), ())), preferred_element_type=jnp.float32
        ),
        "ctx",
        scatter_dimension=0,
        tiled=True,
    )
    all_lse, all_delta = (
        lax.all_gather(jnp.transpose(row_lse), "ctx", axis=0, tiled=True),
        lax.all_gather(jnp.transpose(row_delta), "ctx", axis=0, tiled=True),
    )

    def query_tile(running, tile_in):
        acc_dkey, acc_dvalue = running
        query_t, dout_t, segment_t, lse_t, delta_t = tile_in
        visible = my_segments[None, :, None] <= segment_t[None, None, :]
        scores = (
            jnp.einsum("khd,qhd->hkq", key_heads, query_t, preferred_element_type=jnp.float32)
            * scaling
        )
        probs = jnp.exp(jnp.where(visible, scores - jnp.transpose(lse_t)[:, None, :], NEG_FILL))
        acc_dvalue = acc_dvalue + jnp.einsum(
            "hkq,qhd->hkd", probs.astype(jnp.bfloat16), dout_t, preferred_element_type=jnp.float32
        )
        grad_prob = jnp.einsum(
            "khd,qhd->hkq", value_heads, dout_t, preferred_element_type=jnp.float32
        )
        grad_score = (probs * (grad_prob - jnp.transpose(delta_t)[:, None, :])).astype(jnp.bfloat16)
        acc_dkey = acc_dkey + jnp.einsum(
            "hkq,qhd->hkd", grad_score, query_t, preferred_element_type=jnp.float32
        )
        return (acc_dkey, acc_dvalue)

    def query_step(running, tile_in):
        return (query_tile(running, tile_in), None)

    running = (zeros_acc, zeros_acc)
    query_piece = lax.all_gather(queries, "ctx", axis=0, tiled=True)
    dout_piece = lax.all_gather(grad_attn, "ctx", axis=0, tiled=True)
    length = query_piece.shape[0]
    segment_piece = segment_ids(jnp.int32(0), length, half_rows, block_order, seg_ends)
    tiles = (
        split_tiles(query_piece.reshape(length, heads, HD), length),
        split_tiles(dout_piece.reshape(length, heads, HD), length),
        split_tiles(segment_piece, length),
        split_tiles(all_lse, length),
        split_tiles(all_delta, length),
    )
    running, unused = lax.scan(query_step, running, tiles)
    acc_dkey, acc_dvalue = running
    grad_keys = to_rows(scaling * acc_dkey).astype(jnp.bfloat16)
    grad_values = to_rows(acc_dvalue).astype(jnp.bfloat16)
    return (
        projected,
        to_rows(grad_query).astype(jnp.bfloat16),
        grad_keys,
        grad_values,
        grad_weight,
    )


def solution(mesh):
    return jax.shard_map(
        per_device,
        mesh=mesh,
        in_specs=(
            P("ctx", "head"),
            P("ctx", "head"),
            P("ctx", "head"),
            P(None, "head"),
            P("ctx", "head"),
            P(),
            P(),
        ),
        out_specs=(
            P("ctx", "head"),
            P("ctx", "head"),
            P("ctx", "head"),
            P("ctx", "head"),
            P("ctx", "head"),
        ),
        check_vma=False,
    )
```

profile of v0, /device:TPU:2, one launch (start us, length us, event | category | flops | bytes accessed | tf_op | source)
XLA Modules:
  0.0 650.4 jit_solution(14394680179745567176)
XLA Ops:
  8.7 14.0 %all_gather.23 = bf16[128,3072]{1,0:T(8,128)(2,1)S(1)} all-gather(bf16[128,768]{1,0:T(8,128)(2,1)} %param.15), channel_id=1, replica_groups=mesh['ctx'=64,'head'=4] {'head'}, dimensions={1}, use_global_device_ids=true | all-gather | bytes 983040 | tf_op jit(solution)/shard_map/all_gather | solution.py:38
  30.1 3.2 select_reduce_fusion
  34.3 59.4 %all-gather.5.cloned.1.call-done = bf16[8192,384]{1,0:T(8,128)(2,1)} async-done(((bf16[128,384]{1,0:T(8,128)(2,1)}), bf16[8192,384]{1,0:T(8,128)(2,1)}) %all-gather.5.cloned.1.call-update) | async-done | bytes 6291472 | tf_op jit(solution)/shard_map/all_gather | solution.py:90
  93.6 16.7 %reshape.212 = bf16[16,512,3,128]{3,2,1,0:T(4,128)(2,1)} reshape(bf16[8192,384]{1,0:T(8,128)(2,1)} %all-gather.5.cloned.1.call-done) | data formatting | bytes 12582912 | tf_op jit(solution)/shard_map/reshape;reshape | solution.py:27
  110.3 7.8 %copy.92 = bf16[16,512,3,128]{3,1,2,0:T(8,128)(2,1)} copy(bf16[16,512,3,128]{3,2,1,0:T(4,128)(2,1)} %reshape.212) | data formatting | bytes 12582912
  118.1 56.0 %all-gather.7.cloned.1.call-done = bf16[8192,384]{1,0:T(8,128)(2,1)} async-done(((bf16[128,384]{1,0:T(8,128)(2,1)}), bf16[8192,384]{1,0:T(8,128)(2,1)}) %all-gather.7.cloned.1.call-update) | async-done | bytes 6291472 | tf_op jit(solution)/shard_map/all_gather | solution.py:91
  174.1 16.7 %reshape.213 = bf16[16,512,3,128]{3,2,1,0:T(4,128)(2,1)} reshape(bf16[8192,384]{1,0:T(8,128)(2,1)} %all-gather.7.cloned.1.call-done) | data formatting | bytes 12582912 | tf_op jit(solution)/shard_map/reshape;reshape | solution.py:27
  190.8 7.7 %copy.94 = bf16[16,512,3,128]{3,1,2,0:T(8,128)(2,1)} copy(bf16[16,512,3,128]{3,2,1,0:T(4,128)(2,1)} %reshape.213) | data formatting | bytes 12582912
  198.5 141.4 %while.32 = (s32[]{:T(128)}, f32[3,128]{1,0:T(4,128)S(1)}, f32[3,128]{1,0:T(4,128)}, f32[3,128,128]{2,1,0:T(8,128)S(1)}, f32[3,128,128]{2,1,0:T(8,128)}, /*index...) while((s32[]{:T(128)}, f32[3,128]{1,0:T(4,128)S(1)}, ...), condition=%wide.region_8.9_spmd.clone, body=%wide.region_5.8_spmd.clone.sunk | while | flops 255314176 | bytes 7720143 | solution.py:99
  211.4 2.4 fusion.115
  220.2 2.4 fusion.115
  229.1 2.4 fusion.115
  237.9 2.4 fusion.115
  246.8 2.5 fusion.115
  264.4 2.4 fusion.115
  273.3 2.4 fusion.115
  290.9 2.4 fusion.115
  299.8 2.4 fusion.115
  308.6 2.4 fusion.115
  317.5 2.5 fusion.115
  326.5 2.4 fusion.115
  335.3 2.4 fusion.115
  346.1 16.7 %reshape.215 = bf16[16,512,3,128]{3,2,1,0:T(4,128)(2,1)} reshape(bf16[8192,384]{1,0:T(8,128)(2,1)} %all-gather.11.cloned.1.call-done) | data formatting | bytes 12582912 | tf_op jit(solution)/shard_map/reshape;reshape | solution.py:27
  362.8 7.7 %copy.105 = bf16[16,512,3,128]{3,1,2,0:T(8,128)(2,1)} copy(bf16[16,512,3,128]{3,2,1,0:T(4,128)(2,1)} %reshape.215) | data formatting | bytes 12582912
  370.6 16.7 %reshape.214 = bf16[16,512,3,128]{3,2,1,0:T(4,128)(2,1)} reshape(bf16[8192,384]{1,0:T(8,128)(2,1)} %all-gather.9.cloned.1.call-done) | data formatting | bytes 12582912 | tf_op jit(solution)/shard_map/reshape;reshape | solution.py:27
  387.2 7.9 %copy.103 = bf16[16,512,3,128]{3,1,2,0:T(8,128)(2,1)} copy(bf16[16,512,3,128]{3,2,1,0:T(4,128)(2,1)} %reshape.214) | data formatting | bytes 12582912
  395.2 2.9 convolution_bitcast_fusion.1
  398.1 6.0 copy.126
  404.2 48.2 %all_gather.27 = f32[8192,3]{0,1:T(4,128)S(1)} all-gather(f32[128,3]{0,1:T(4,128)S(1)} %bitcast.158), channel_id=1, replica_groups=mesh['ctx'=64,'head'=4] {'ctx'}, dimensions={0}, use_global_device_ids=true | all-gather | bytes 99840 | tf_op jit(solution)/shard_map/all_gather | solution.py:129
  452.4 47.7 %all_gather.25 = f32[8192,3]{0,1:T(4,128)S(1)} all-gather(f32[128,3]{0,1:T(4,128)S(1)} %get-tuple-element.367), channel_id=1, replica_groups=mesh['ctx'=64,'head'=4] {'ctx'}, dimensions={0}, use_global_device_ids=true | all-gather | bytes 99840 | tf_op jit(solution)/shard_map/all_gather | solution.py:128
  500.2 85.9 %while.33 = (s32[]{:T(128)}, f32[3,128,128]{2,1,0:T(8,128)S(1)}, f32[3,128,128]{2,1,0:T(8,128)S(1)}, s32[128]{0:T(128)}, s32[16,512]{1,0:T(8,128)S(1)}, /*index=...) while((s32[]{:T(128)}, f32[3,128,128]{2,1,0:T(8,128)S(1)}, ...), condition=%wide.region_12.13_spmd.clone, body=%wide.region_11.12_spmd.clone.sunk | while | flops 202964992 | bytes 5091984 | solution.py:168
  589.0 54.6 %reduce-scatter.7.cloned.1.call-done = f32[48,384]{1,0:T(8,128)} async-done(((f32[3072,384]{1,0:T(8,128)}), f32[48,384]{1,0:T(8,128)}) %reduce-scatter.7.cloned.1.call-update) | async-done | bytes 73744
  (374 shorter events, 212.0 us)
Async XLA Ops:
  7.2 16.5 %copy-start = (bf16[3072,384]{1,0:T(8,128)(2,1)S(1)}, bf16[3072,384]{1,0:T(8,128)(2,1)}, u32[]{:S(2)}) copy-start(bf16[3072,384]{1,0:T(8,128)(2,1)} %param.14) | copy-start | bytes 7077892
  7.2 86.4 %all-gather.5.cloned.1.call-start = ((), (), s32[]{:S(2)}) async-start(), calls=%async_computation.2 | async-start | bytes 6389760 | tf_op jit(solution)/shard_map/all_gather | solution.py:90
  7.9 166.2 %all-gather.7.cloned.1.call-start = ((), (), s32[]{:S(2)}) async-start(), calls=%async_computation.3 | async-start | bytes 6389760 | tf_op jit(solution)/shard_map/all_gather | solution.py:91
  8.7 337.4 %all-gather.11.cloned.1.call-start = ((), (), s32[]{:S(2)}) async-start(), calls=%async_computation.6 | async-start | bytes 6389760 | tf_op jit(solution)/shard_map/all_gather | solution.py:158
  22.8 0.9 copy-start.2
  24.9 345.7 %all-gather.9.cloned.1.call-start = ((), (), s32[]{:S(2)}) async-start(), calls=%async_computation.5 | async-start | bytes 6389760 | tf_op jit(solution)/shard_map/all_gather | solution.py:157
  25.5 563.5 %reduce-scatter.5.cloned.1.call-start = ((), (), s32[]{:S(2)}) async-start(), calls=%async_computation.4 | async-start | bytes 983040 | tf_op jit(solution)/shard_map/reduce_scatter | solution.py:116
  26.5 83.8 %copy-start.5 = (bf16[128,384]{0,1:T(8,128)(2,1)}, bf16[128,384]{0,1:T(8,128)(2,1)S(1)}, u32[]{:S(2)}) copy-start(bf16[128,384]{0,1:T(8,128)(2,1)S(1)} %copy.91) | copy-start | bytes 294916
  200.6 6.0 copy-start.7
  206.6 0.6 copy-start.8
  209.3 6.1 copy-start.7
  218.1 6.1 copy-start.7
  227.0 6.1 copy-start.7
  235.8 6.1 copy-start.7
  244.6 6.2 copy-start.7
  250.8 0.6 copy-start.8
  253.5 6.1 copy-start.7
  262.3 6.1 copy-start.7
  268.5 0.6 copy-start.8
  271.2 6.1 copy-start.7
  280.0 6.1 copy-start.7
  288.8 6.1 copy-start.7
  297.6 6.1 copy-start.7
  306.5 6.2 copy-start.7
  315.4 6.3 copy-start.7
  324.4 6.1 copy-start.7
  333.2 6.1 copy-start.7
  343.5 300.1 %reduce-scatter.7.cloned.1.call-start = ((), (), s32[]{:S(2)}) async-start(), calls=%async_computation.7 | async-start | bytes 4792320
  387.2 7.9 %copy-start.3 = (bf16[128,3072]{1,0:T(8,128)(2,1)S(1)}, bf16[128,3072]{1,0:T(8,128)(2,1)}, u32[]{:S(2)}) copy-start(bf16[128,3072]{1,0:T(8,128)(2,1)} %copy-done.2) | copy-start | bytes 2359300
  500.1 86.0 %copy-start.4 = (f32[3,128,128]{2,1,0:T(8,128)S(1)}, f32[3,128,128]{2,1,0:T(8,128)}, u32[]{:S(2)}) copy-start(f32[3,128,128]{2,1,0:T(8,128)} %get-tuple-element.132) | copy-start | bytes 589828
  500.1 86.1 %copy-start.6 = (f32[3,128,128]{2,1,0:T(8,128)S(1)}, f32[3,128,128]{2,1,0:T(8,128)}, u32[]{:S(2)}) copy-start(f32[3,128,128]{2,1,0:T(8,128)} %get-tuple-element.131) | copy-start | bytes 589828
  586.1 57.5 %copy-start.1 = (bf16[3072,384]{1,0:T(8,128)(2,1)S(1)}, bf16[3072,384]{1,0:T(8,128)(2,1)}, u32[]{:S(2)}) copy-start(bf16[3072,384]{1,0:T(8,128)(2,1)} %param.14) | copy-start | bytes 7077892
  (13 other events, 7.6 us)
Sparse Core Ops, SparseCore 0:
  10.8 82.8 all-gather.4
  96.4 77.6 all-gather.6
  177.4 77.6 all-gather.10
  257.7 77.6 all-gather.8
  343.7 23.0 reduce-scatter.4
  500.3 143.2 reduce-scatter.6
where the time goes:
time: 657 us; the launch traced here: 650 us
  matrix products  194 us (30%)
  waiting for transfers between devices  172 us (26%)
  local copies, waits for them, and re-layouts  123 us (19%)
  blocking collectives  110 us (17%)
  other arithmetic  34.8 us (5%)
  between operations  14.4 us (2%)
    another operation x4, local copies, waits for them, and re-layouts, split_tiles(): return array_in.reshape((length // tile_len, tile_len) + array_in.shape[1:])  66.7 us
    all_gather x1, waiting for transfers between devices, per_device(): key_piece = lax.all_gather(key_rows, 'ctx', axis=0, tiled=True)  59.4 us
    unnamed x7, waiting for transfers between devices  56.6 us
    all_gather x1, waiting for transfers between devices, per_device(): value_piece = lax.all_gather(value_rows, 'ctx', axis=0, tiled=True)  56 us
    all_gather x1, blocking collectives, per_device(): lax.all_gather(jnp.transpose(row_delta), 'ctx', axis=0, tiled=True)  48.2 us
    all_gather x1, blocking collectives, per_device(): lax.all_gather(jnp.transpose(row_lse), 'ctx', axis=0, tiled=True)  47.7 us
    unnamed x29, local copies, waits for them, and re-layouts  44.7 us
    dot_general x16, matrix products, key_tile(): jnp.einsum('hqk,khd->hqd', (weights * grad_prob).astype(jnp.bfloat16), ke...  39.1 us
  transfers between devices with their start and end apart: 6, of which 3 were waited for; matrix products, arithmetic and copies ran while one was open for 53% of the time, Pallas kernels for 0%

commit v1 on v0

v1 whole, which is shorter than its diff:
```python
import functools
import math

import jax
import jax.numpy as jnp
from jax import lax
from jax.experimental import pallas as pl
from jax.experimental.pallas import tpu as pltpu
from jax.sharding import PartitionSpec as P

HD = 128
HEADS = 3
TOK = 128
WID = HEADS * HD
BLK = 64
SEGS = 8
SCALE = 1.0 / math.sqrt(HD)
EXP2_SCALE = SCALE * math.log2(math.e)
NEG_FILL = -1e30
MAX_FLOOR = -1e20
F32 = jnp.float32
BF16 = jnp.bfloat16
MESH = pl.DeviceIdType.MESH


def dot_nn(a, b):
    return jnp.dot(a, b, preferred_element_type=F32)


def dot_nt(a, b):
    return lax.dot_general(a, b, (((1,), (1,)), ((), ())), preferred_element_type=F32)


def dot_tn(a, b):
    return lax.dot_general(a, b, (((0,), (0,)), ((), ())), preferred_element_type=F32)


def head_lanes(h):
    return pl.ds(pl.multiple_of(h * HD, HD), HD)


def kernel(
    X, Z, Y,
    seg_len, order, q_in, k_in, v_in, w_in, gp_in,
    proj_out, dq_out, dk_out, dv_out, gw_out,
    qb, db, kvb, gpf, gpx, segk, segq, pbuf, dpbuf, mst, lst, dst,
    oacc, mrun, st_send, st_recv, o_send, o_recv, attb, dqacc, dq_send, dq_recv,
    pj_send, pj_recv, fac, delta, part, sib_recv, rs_send, rs_recv,
    gwf, gwp, g_sib, g_send, g_recv,
    x_ss, x_rs, y_ss, y_rs, ring_ss, ring_rs, ksib_ss, ksib_rs,
    sib_ss, sib_rs, rs_ss, rs_rs, gsib_ss, gsib_rs, g_ss, g_rs,
):
    nplus, nminus = Z // 2, Z - 1 - Z // 2
    QN = X * TOK
    gcols = gp_in.shape[1]
    me = lax.axis_index("ctx")
    y = lax.axis_index("head")
    core = lax.rem(me, 2)
    z = lax.rem(me // 2, Z)
    x = me // (2 * Z)

    def ctx_of(xx, zz, cc):
        return (xx * Z + zz) * 2 + cc

    def zmod(off):
        return lax.rem(z + off + 2 * Z, Z)

    other = 1 - core
    sib = (ctx_of(x, z, other), y)
    up = (ctx_of(x, zmod(1), core), y)
    down = (ctx_of(x, zmod(-1), core), y)

    def x_dev(i):
        return (ctx_of(lax.rem(x + i, X), z, core), y)

    def y_dev(i):
        return (me, lax.rem(y + i, Y))

    def rcopy(src, dst_ref, ss, rs, dev):
        return pltpu.make_async_remote_copy(
            src_ref=src, dst_ref=dst_ref, send_sem=ss, recv_sem=rs,
            device_id=dev, device_id_type=MESH,
        )

    barrier = pltpu.get_barrier_semaphore()
    partners = [up, down, sib]
    partners += [x_dev(i) for i in range(1, X)] + [y_dev(i) for i in range(1, Y)]
    for dev in partners:
        pl.semaphore_signal(barrier, inc=1, device_id=dev, device_id_type=MESH)
    pl.semaphore_wait(barrier, len(partners))

    sends = []

    def go(copy):
        copy.start()
        sends.append(copy)

    def x_recv(kind, i, buf):
        slot = buf.at[lax.rem(x + X - i, X)]
        rcopy(slot, slot, x_ss.at[kind, i], x_rs.at[kind, i], x_dev(i)).wait_recv()

    def x_send(kind, i, src, buf):
        go(rcopy(src, buf.at[x], x_ss.at[kind, i], x_rs.at[kind, i], x_dev(i)))

    def y_recv(kind, i, buf):
        slot = buf.at[lax.rem(y + Y - i, Y)]
        rcopy(slot, slot, y_ss.at[kind, i], y_rs.at[kind, i], y_dev(i)).wait_recv()

    def y_send(kind, i, src, buf):
        go(rcopy(src, buf.at[y], y_ss.at[kind, i], y_rs.at[kind, i], y_dev(i)))

    def kv_slot(off, cc, a):
        return kvb.at[zmod(off), cc, a]

    def ring_send(direction, step, a, src):
        off = 1 - step if direction == 0 else step - 1
        go(rcopy(
            src, kv_slot(off, core, a),
            ring_ss.at[direction, step - 1, a], ring_rs.at[direction, step - 1, a],
            up if direction == 0 else down,
        ))

    def ring_wait(direction, step, a):
        off = -step if direction == 0 else step
        slot = kv_slot(off, core, a)
        rcopy(
            slot, slot, ring_ss.at[direction, step - 1, a],
            ring_rs.at[direction, step - 1, a], up,
        ).wait_recv()

    def sib_index(off):
        return nplus + off if off > 0 else -off

    def ksib_send(off, a, src):
        j = sib_index(off)
        go(rcopy(src, kv_slot(off, core, a), ksib_ss.at[j, a], ksib_rs.at[j, a], sib))

    def ksib_wait(off, a):
        j = sib_index(off)
        slot = kv_slot(off, other, a)
        rcopy(slot, slot, ksib_ss.at[j, a], ksib_rs.at[j, a], sib).wait_recv()

    for i in range(1, Y):
        y_send(0, i, gp_in, gpf)
    for a, src in ((0, k_in), (1, v_in)):
        ring_send(0, 1, a, src)
        if nminus >= 1:
            ring_send(1, 1, a, src)
        ksib_send(0, a, src)
    for i in range(1, X):
        x_send(0, i, q_in, qb)
    qb[x] = q_in[...]
    kvb[z, core, 0] = k_in[...]
    kvb[z, core, 1] = v_in[...]

    ends = []
    total = seg_len[0]
    for i in range(SEGS - 1):
        ends.append(total)
        total = total + seg_len[i + 1]

    def segments(row_in_block, ctx_id):
        first = order[2 * ctx_id] * BLK
        second = order[2 * ctx_id + 1] * BLK - BLK
        pos = row_in_block + jnp.where(row_in_block < BLK, first, second)
        seg = jnp.zeros_like(pos)
        for end in ends:
            seg = seg + jnp.where(pos >= end, 1, 0)
        return seg

    lanes = lax.broadcasted_iota(jnp.int32, (1, TOK), 1)
    for xx in range(X):
        segq[:, xx * TOK:(xx + 1) * TOK] = segments(lanes, ctx_of(xx, z, core))
    rows = lax.broadcasted_iota(jnp.int32, (TOK, 128), 0)

    def seg_body(zz, carry):
        for cc in range(2):
            segk[zz, cc * TOK:(cc + 1) * TOK, :] = segments(rows, ctx_of(x, zz, cc))
        return carry

    lax.fori_loop(0, Z, seg_body, 0)
    for h in range(HEADS):
        mrun[h] = jnp.full((1, QN), MAX_FLOOR, F32)
        oacc[h] = jnp.zeros((HD, QN), F32)
        dqacc[h] = jnp.zeros((HD, QN), F32)

    def keys(zi, a, h):
        return kvb[zi, :, a, :, head_lanes(h)].reshape(2 * TOK, HD)

    def gathered(buf, h):
        return buf[:, :, head_lanes(h)].reshape(QN, HD)

    def fwd(zi):
        def body(h, carry):
            s = dot_nt(keys(zi, 0, h), gathered(qb, h))
            sk = jnp.concatenate([segk[zi]] * X, axis=1)
            s = jnp.where(sk <= segq[...], s, NEG_FILL)
            m = jnp.maximum(jnp.max(s, axis=0, keepdims=True), MAX_FLOOR)
            p = jnp.exp2((s - m) * EXP2_SCALE)
            pbuf[h, zi] = p
            mst[h, zi] = m
            lst[h, zi] = jnp.sum(p, axis=0, keepdims=True)
            pv = dot_tn(keys(zi, 1, h), p.astype(BF16))
            m_old = mrun[h]
            m_new = jnp.maximum(m_old, m)
            mrun[h] = m_new
            oacc[h] = (
                oacc[h] * jnp.exp2((m_old - m_new) * EXP2_SCALE)
                + pv * jnp.exp2((m - m_new) * EXP2_SCALE)
            )
            return carry

        lax.fori_loop(0, HEADS, body, 0)

    def dprob(zi):
        def body(h, carry):
            dp = dot_nt(keys(zi, 1, h), gathered(db, h))
            dpbuf[h, zi] = dp
            dst[h, zi] = jnp.sum(dp * pbuf[h, zi], axis=0, keepdims=True)
            return carry

        lax.fori_loop(0, HEADS, body, 0)

    def ring_step(step):
        for a in range(2):
            ring_wait(0, step, a)
            if step < nplus:
                ring_send(0, step + 1, a, kv_slot(-step, core, a))
            ksib_send(-step, a, kv_slot(-step, core, a))
            if step <= nminus:
                ring_wait(1, step, a)
                if step < nminus:
                    ring_send(1, step + 1, a, kv_slot(step, core, a))
                ksib_send(step, a, kv_slot(step, core, a))

    def step_offsets(step):
        return [0] if step == 0 else ([-step, step] if step <= nminus else [-step])

    def sib_ready(step):
        for off in step_offsets(step):
            for a in range(2):
                ksib_wait(off, a)

    def over(step, fn):
        offs = step_offsets(step)
        if len(offs) == 1:
            fn(zmod(offs[0]))
        else:
            def body(i, carry):
                fn(zmod(step * (2 * i - 1)))
                return carry

            lax.fori_loop(0, 2, body, 0)

    acc = None
    for i in range(Y):
        if i:
            y_recv(0, i, gpf)
        src_y = lax.rem(y + Y - i, Y)
        if i == 0:
            gpf[src_y] = gp_in[...]
        w_rows = w_in[pl.ds(pl.multiple_of(src_y * gcols, gcols), gcols), :]
        term = dot_nn(gpf[src_y], w_rows)
        acc = term if acc is None else acc + term
        if i == 0:
            ring_step(1)
    db[x] = acc.astype(BF16)
    for i in range(1, X):
        x_send(1, i, db.at[x], db)
    for i in range(1, X):
        x_send(2, i, gpf.at[lax.rem(x + i, X)], gpx)
    gpx[x] = gpf[x]

    for i in range(1, X):
        x_recv(0, i, qb)
    sib_ready(0)
    over(0, fwd)
    done = [0]
    have_dout = False
    for step in range(1, nplus + 1):
        sib_ready(step)
        if step < nplus:
            ring_step(step + 1)
        over(step, fwd)
        done.append(step)
        if step >= 2 and not have_dout:
            have_dout = True
            for i in range(1, X):
                x_recv(1, i, db)
            for prev in done:
                over(prev, dprob)
        elif have_dout:
            over(step, dprob)

    for h in range(HEADS):
        m_all, l_all, d_all = mst[h], lst[h], dst[h]
        m_top = mrun[h]
        w = jnp.exp2((m_all - m_top[None]) * EXP2_SCALE)
        l_sum = jnp.maximum(jnp.sum(l_all * w, axis=0), 1e-30)
        inv = 1.0 / l_sum
        st_send[h:h + 1, :] = m_top * EXP2_SCALE + jnp.log2(l_sum)
        st_send[HEADS + h:HEADS + h + 1, :] = jnp.sum(d_all * w, axis=0) * inv
        o_h = (oacc[h] * inv).astype(BF16)
        for xx in range(X):
            o_send[xx, h * HD:(h + 1) * HD, :] = o_h[:, xx * TOK:(xx + 1) * TOK]
    st_send[2 * HEADS:8, :] = jnp.zeros((8 - 2 * HEADS, QN), F32)
    for i in range(1, X):
        x_send(3, i, st_send, st_recv)
    for i in range(1, X):
        x_send(4, i, o_send.at[lax.rem(x + i, X)], o_recv)
    st_recv[x] = st_send[...]
    o_recv[x] = o_send[x]
    for i in range(1, X):
        x_recv(3, i, st_recv)
    lse_all = st_recv[:, 0:HEADS, :]
    top = jnp.max(lse_all, axis=0)
    lse = top + jnp.log2(jnp.sum(jnp.exp2(lse_all - top[None]), axis=0))
    weight = jnp.exp2(lse_all - lse[None])
    delta_all = jnp.sum(weight * st_recv[:, HEADS:2 * HEADS, :], axis=0)
    for h in range(HEADS):
        delta[h] = delta_all[h:h + 1]
        fac[h] = jnp.exp2(mst[h] * EXP2_SCALE - lse[h:h + 1][None])
    own_stats = st_recv[:, 0:HEADS, pl.ds(pl.multiple_of(x * TOK, TOK), TOK)]
    own_top = jnp.max(own_stats, axis=0)
    own_w = jnp.exp2(own_stats - own_top[None])
    own_w = own_w / jnp.sum(own_w, axis=0)[None]

    def dest_off(o):
        half = o // 2
        return jnp.where(lax.rem(o, 2) == 0, nplus - half, half - nminus)

    def bwd(o):
        zi = zmod(dest_off(o))

        def body(h, carry):
            lanes_h = head_lanes(h)
            p = pbuf[h, zi] * fac[h, zi]
            ds = (p * (dpbuf[h, zi] - delta[h])).astype(BF16)
            dv = dot_nn(p.astype(BF16), gathered(db, h)).astype(BF16)
            dk = (dot_nn(ds, gathered(qb, h)) * SCALE).astype(BF16)
            for cc in range(2):
                part[o, cc, 0, :, lanes_h] = dk[cc * TOK:(cc + 1) * TOK]
                part[o, cc, 1, :, lanes_h] = dv[cc * TOK:(cc + 1) * TOK]
            dqacc[h] = dqacc[h] + dot_tn(keys(zi, 0, h), ds)
            return carry

        lax.fori_loop(0, HEADS, body, 0)

    def sib_copy(o):
        return rcopy(part.at[o, other], sib_recv.at[o], sib_ss.at[o], sib_rs.at[o], sib)

    def ring_dev(o):
        zz = jnp.where(lax.rem(o, 2) == 0, zmod(1), zmod(-1))
        return (ctx_of(x, zz, core), y)

    def rs_copy(o):
        return rcopy(rs_send.at[o], rs_recv.at[o + 2], rs_ss.at[o], rs_rs.at[o + 2], ring_dev(o))

    def rs_wait(o):
        slot = rs_recv.at[o]
        rcopy(slot, slot, rs_ss.at[0], rs_rs.at[o], up).wait_recv()

    def finalize(o):
        sib_copy(o).wait_recv()
        for a in range(2):
            rs_send[o, a] = (
                part[o, core, a].astype(F32) + sib_recv[o, a].astype(F32)
            ).astype(BF16)

        @pl.when(o >= 2)
        def _():
            rs_wait(o)
            for a in range(2):
                rs_send[o, a] = (
                    part[o, core, a].astype(F32)
                    + sib_recv[o, a].astype(F32)
                    + rs_recv[o, a].astype(F32)
                ).astype(BF16)

        rs_copy(o).start()

    def bwd_range(first, last):
        def body(o, carry):
            bwd(o)
            sib_copy(o).start()
            finalize(o - 1)
            return carry

        lax.fori_loop(first, last, body, 0)

    cut_a, cut_b = max(1, Z // 4), max(2, Z // 2 + 1)
    bwd(0)
    sib_copy(0).start()
    bwd_range(1, cut_a)

    for i in range(1, X):
        x_recv(4, i, o_recv)
    for h in range(HEADS):
        o_t = jnp.zeros((HD, TOK), F32)
        for xx in range(X):
            o_t = o_t + o_recv[xx, h * HD:(h + 1) * HD, :].astype(F32) * own_w[xx, h:h + 1]
        attb[x, :, h * HD:(h + 1) * HD] = o_t.T.astype(BF16)
    for i in range(1, X):
        x_send(5, i, attb.at[x], attb)
    att = attb[x]
    for i in range(1, Y):
        dst_y = lax.rem(y + i, Y)
        w_rows = w_in[pl.ds(pl.multiple_of(dst_y * gcols, gcols), gcols), :]
        pj_send[dst_y] = dot_nt(att, w_rows).astype(BF16)
        y_send(1, i, pj_send.at[dst_y], pj_recv)
    w_rows = w_in[pl.ds(pl.multiple_of(y * gcols, gcols), gcols), :]
    pj_recv[y] = dot_nt(att, w_rows).astype(BF16)

    bwd_range(cut_a, cut_b)

    for i in range(1, X):
        x_recv(2, i, gpx)
    for i in range(1, X):
        x_recv(5, i, attb)
    att_all = attb[...].reshape(QN, WID)

    def gw_body(j, carry):
        lanes_j = pl.ds(pl.multiple_of(j * 128, 128), 128)
        left = gpx[:, :, lanes_j].reshape(QN, 128)
        gwf[pl.ds(pl.multiple_of(j * 128, 128), 128), :] = dot_tn(left, att_all)
        return carry

    lax.fori_loop(0, gcols // 128, gw_body, 0)
    grow = gw_out.shape[0]
    for zz in range(Z):
        for cc in range(2):
            first = (zz * 2 + cc) * grow
            gwp[cc, zz] = gwf[first:first + grow, :].astype(BF16)
    gsib = rcopy(gwp.at[other], g_sib, gsib_ss, gsib_rs, sib)
    go(gsib)

    bwd_range(cut_b, Z)

    for h in range(HEADS):
        dq_h = (dqacc[h] * SCALE).astype(BF16)
        for xx in range(X):
            dq_send[xx, h * HD:(h + 1) * HD, :] = dq_h[:, xx * TOK:(xx + 1) * TOK]
    for i in range(1, X):
        x_send(6, i, dq_send.at[lax.rem(x + i, X)], dq_recv)
    dq_recv[x] = dq_send[x]

    gsib.wait_recv()

    def g_copy(o):
        return rcopy(g_send.at[o], g_recv.at[o + 2], g_ss.at[o], g_rs.at[o + 2], ring_dev(o))

    def g_wait(o):
        slot = g_recv.at[o]
        rcopy(slot, slot, g_ss.at[0], g_rs.at[o], up).wait_recv()

    def g_term(zi):
        return gwp[core, zi].astype(F32) + g_sib[zi].astype(F32)

    def g_body(o, carry):
        zi = zmod(dest_off(o))
        g_send[o] = g_term(zi).astype(BF16)

        @pl.when(o >= 2)
        def _():
            g_wait(o)
            g_send[o] = (g_term(zi) + g_recv[o].astype(F32)).astype(BF16)

        g_copy(o).start()
        return carry

    lax.fori_loop(0, Z - 1, g_body, 0)

    for i in range(1, Y):
        y_recv(1, i, pj_recv)
    proj = pj_recv[0].astype(F32)
    for yy in range(1, Y):
        proj = proj + pj_recv[yy].astype(F32)
    proj_out[...] = proj.astype(BF16)
    for i in range(1, X):
        x_recv(6, i, dq_recv)
    for h in range(HEADS):
        dq_t = jnp.zeros((HD, TOK), F32)
        for xx in range(X):
            dq_t = dq_t + dq_recv[xx, h * HD:(h + 1) * HD, :].astype(F32)
        dq_out[:, h * HD:(h + 1) * HD] = dq_t.T.astype(BF16)
    last = Z - 1
    sib_copy(last).wait_recv()
    rs_wait(last)
    rs_wait(last + 1)
    for a, out in ((0, dk_out), (1, dv_out)):
        out[...] = (
            part[last, core, a].astype(F32)
            + sib_recv[last, a].astype(F32)
            + rs_recv[last, a].astype(F32)
            + rs_recv[last + 1, a].astype(F32)
        ).astype(BF16)
    g_wait(last)
    g_wait(last + 1)
    gw_out[...] = g_term(z) + g_recv[last].astype(F32) + g_recv[last + 1].astype(F32)

    for copy in sends:
        copy.wait_send()

    def drain(o, carry):
        sib_copy(o).wait_send()
        rs_copy(o).wait_send()
        g_copy(o).wait_send()
        return carry

    lax.fori_loop(0, Z - 1, drain, 0)
    sib_copy(last).wait_send()


def per_device(X, Z, Y, queries, key_rows, value_rows, out_weight, grad_projected, segment_len, block_order):
    gcols = grad_projected.shape[1]
    grow = out_weight.shape[0] // (X * Z * 2)
    QN = X * TOK
    vmem = pl.BlockSpec(memory_space=pltpu.VMEM)
    smem = pl.BlockSpec(memory_space=pltpu.SMEM)
    dma = pltpu.SemaphoreType.DMA
    scratch = [
        pltpu.VMEM((X, TOK, WID), BF16),
        pltpu.VMEM((X, TOK, WID), BF16),
        pltpu.VMEM((Z, 2, 2, TOK, WID), BF16),
        pltpu.VMEM((Y, TOK, gcols), BF16),
        pltpu.VMEM((X, TOK, gcols), BF16),
        pltpu.VMEM((Z, 2 * TOK, 128), jnp.int32),
        pltpu.VMEM((1, QN), jnp.int32),
        pltpu.VMEM((HEADS, Z, 2 * TOK, QN), F32),
        pltpu.VMEM((HEADS, Z, 2 * TOK, QN), F32),
        pltpu.VMEM((HEADS, Z, 1, QN), F32),
        pltpu.VMEM((HEADS, Z, 1, QN), F32),
        pltpu.VMEM((HEADS, Z, 1, QN), F32),
        pltpu.VMEM((HEADS, HD, QN), F32),
        pltpu.VMEM((HEADS, 1, QN), F32),
        pltpu.VMEM((8, QN), F32),
        pltpu.VMEM((X, 8, QN), F32),
        pltpu.VMEM((X, WID, TOK), BF16),
        pltpu.VMEM((X, WID, TOK), BF16),
        pltpu.VMEM((X, TOK, WID), BF16),
        pltpu.VMEM((HEADS, HD, QN), F32),
        pltpu.VMEM((X, WID, TOK), BF16),
        pltpu.VMEM((X, WID, TOK), BF16),
        pltpu.VMEM((Y, TOK, gcols), BF16),
        pltpu.VMEM((Y, TOK, gcols), BF16),
        pltpu.VMEM((HEADS, Z, 1, QN), F32),
        pltpu.VMEM((HEADS, 1, QN), F32),
        pltpu.VMEM((Z, 2, 2, TOK, WID), BF16),
        pltpu.VMEM((Z, 2, TOK, WID), BF16),
        pltpu.VMEM((Z, 2, TOK, WID), BF16),
        pltpu.VMEM((Z + 1, 2, TOK, WID), BF16),
        pltpu.VMEM((gcols, WID), F32),
        pltpu.VMEM((2, Z, grow, WID), BF16),
        pltpu.VMEM((Z, grow, WID), BF16),
        pltpu.VMEM((Z, grow, WID), BF16),
        pltpu.VMEM((Z + 1, grow, WID), BF16),
        dma((7, X)), dma((7, X)),
        dma((2, Y)), dma((2, Y)),
        dma((2, Z // 2, 2)), dma((2, Z // 2, 2)),
        dma((Z, 2)), dma((Z, 2)),
        dma((Z,)), dma((Z,)),
        dma((Z + 1,)), dma((Z + 1,)),
        dma, dma,
        dma((Z + 1,)), dma((Z + 1,)),
    ]
    out_shape = (
        jax.ShapeDtypeStruct((TOK, gcols), BF16),
        jax.ShapeDtypeStruct((TOK, WID), BF16),
        jax.ShapeDtypeStruct((TOK, WID), BF16),
        jax.ShapeDtypeStruct((TOK, WID), BF16),
        jax.ShapeDtypeStruct((grow, WID), F32),
    )
    return pl.pallas_call(
        functools.partial(kernel, X, Z, Y),
        out_shape=out_shape,
        in_specs=[smem, smem, vmem, vmem, vmem, vmem, vmem],
        out_specs=(vmem,) * 5,
        scratch_shapes=scratch,
        compiler_params=pltpu.CompilerParams(
            collective_id=0, has_side_effects=True, vmem_limit_bytes=60 * 1024 * 1024
        ),
        name="segment_attention",
    )(segment_len, block_order, queries, key_rows, value_rows, out_weight, grad_projected)


def solution(mesh):
    ctx = mesh.shape["ctx"]
    Y = mesh.shape["head"]
    X = Y
    Z = ctx // (2 * X)
    return jax.shard_map(
        functools.partial(per_device, X, Z, Y),
        mesh=mesh,
        in_specs=(
            P("ctx", "head"),
            P("ctx", "head"),
            P("ctx", "head"),
            P(None, "head"),
            P("ctx", "head"),
            P(),
            P(),
        ),
        out_specs=(P("ctx", "head"),) * 5,
        check_vma=False,
    )
```

time: 657 us -> 95.4 us (0.15)
  matrix products: 194 us -> 0 us
  waiting for transfers between devices: 172 us -> 0 us
  local copies, waits for them, and re-layouts: 123 us -> 7.76 us
  blocking collectives: 110 us -> 0 us
  Pallas kernels: 0 us -> 86.8 us
  other arithmetic: 34.8 us -> 0 us
  between operations: 14.4 us -> 0.64 us
    dot_general x115 -> x0, matrix products: 194 us -> none  [the longest x16 39.1 us: key_tile(): jnp.einsum('hqk,khd->hqd', (weights * grad_prob).astype(jnp.bfloat16), ke...]
    all_gather x4 -> x0, waiting for transfers between devices: 115 us -> none  [the longest x1 59.4 us: per_device(): key_piece = lax.all_gather(key_rows, 'ctx', axis=0, tiled=True)]
    all_gather x3 -> x0, blocking collectives: 110 us -> none  [the longest x1 48.2 us: per_device(): lax.all_gather(jnp.transpose(row_delta), 'ctx', axis=0, tiled=True)]
    pallas_call x0 -> x1, Pallas kernels: none -> 86.8 us  [per_device(): pl.pallas_call(functools.partial(kernel, X, Z, Y), out_shape=out_shape, i...]
    another operation x4 -> x0, local copies, waits for them, and re-layouts: 66.7 us -> none  [split_tiles(): return array_in.reshape((length // tile_len, tile_len) + array_in.shape[1:])]
    unnamed x7 -> x0, waiting for transfers between devices: 56.6 us -> none
    unnamed x29 -> x5, local copies, waits for them, and re-layouts: 44.7 us -> 7.76 us
    le x32 -> x0, other arithmetic: 24.4 us -> none  [the longest x16 12.3 us: query_tile(): visible = my_segments[None, :, None] <= segment_t[None, None, :]]
  transfers between devices with their start and end apart: 6 -> 0, of which waited for: 3 -> 0; matrix products, arithmetic and copies ran while one was open for 53% -> 0% of each run, Pallas kernels for 0% -> 0%
where the time goes in v1:
time: 95.4 us; the launch traced here: 95.2 us
  Pallas kernels  86.8 us (91%)
  local copies, waits for them, and re-layouts  7.76 us (8%)
    pallas_call x1, Pallas kernels, per_device(): pl.pallas_call(functools.partial(kernel, X, Z, Y), out_shape=out_shape, i...  86.8 us
    unnamed x5, local copies, waits for them, and re-layouts  7.76 us

profile of v1, /device:TPU:2, one launch (start us, length us, event | category | flops | bytes accessed | tf_op | source)
XLA Modules:
  0.0 95.2 jit_solution(4860363707124269405)
XLA Ops:
  0.6 86.8 %segment_attention.1 = (bf16[128,768]{1,0:T(8,128)(2,1)}, bf16[128,384]{1,0:T(8,128)(2,1)}, bf16[128,384]{1,0:T(8,128)(2,1)}, bf16[128,384]{1,0:T(8,128)(2,1)}, f32[48,384]{1,0:T(8,128)}) custom-call(s32[8]{0:T(128)} %seg_len.1, s32[128]{0:T(128)} %order.1, bf16[128,384]{1,0:T(8,128)(2,1)} %q_in.1, bf16[128,384]{1,0:T(8,128)(2,1)} %k_in.1, ...), custom_call_target="tpu_custom_call" | custom-call | tf_op jit(solution)/shard_map/segment_attention/pallas_call | solution.py:573
  87.4 1.6 %copy.17 = bf16[128,768]{1,0:T(8,128)(2,1)} copy(bf16[128,768]{1,0:T(8,128)(2,1)} %get-tuple-element.10) | data formatting | bytes 393216
  89.0 1.5 %copy.18 = bf16[128,384]{1,0:T(8,128)(2,1)} copy(bf16[128,384]{1,0:T(8,128)(2,1)} %get-tuple-element.11) | data formatting | bytes 196608
  90.6 1.5 %copy.19 = bf16[128,384]{1,0:T(8,128)(2,1)} copy(bf16[128,384]{1,0:T(8,128)(2,1)} %get-tuple-element.12) | data formatting | bytes 196608
  92.1 1.5 %copy.20 = bf16[128,384]{1,0:T(8,128)(2,1)} copy(bf16[128,384]{1,0:T(8,128)(2,1)} %get-tuple-element.13) | data formatting | bytes 196608
  93.6 1.5 %copy.21 = f32[48,384]{1,0:T(8,128)} copy(f32[48,384]{1,0:T(8,128)} %get-tuple-element.14) | data formatting | bytes 147456

commit v2 on v1

v2 whole, which is shorter than its diff:
```python
import functools
import math

import jax
import jax.numpy as jnp
from jax import lax
from jax.experimental import pallas as pl
from jax.experimental.pallas import tpu as pltpu
from jax.sharding import PartitionSpec as P

HD = 128
HEADS = 3
TOK = 128
WID = HEADS * HD
BLK = 64
SEGS = 8
SCALE = 1.0 / math.sqrt(HD)
EXP2_SCALE = SCALE * math.log2(math.e)
NEG_FILL = -1e30
MAX_FLOOR = -1e20
F32 = jnp.float32
BF16 = jnp.bfloat16
MESH = pl.DeviceIdType.MESH


def dot_nn(a, b):
    return jnp.dot(a, b, preferred_element_type=F32)


def dot_nt(a, b):
    return lax.dot_general(a, b, (((1,), (1,)), ((), ())), preferred_element_type=F32)


def dot_tn(a, b):
    return lax.dot_general(a, b, (((0,), (0,)), ((), ())), preferred_element_type=F32)


def head_lanes(h):
    return slice(h * HD, (h + 1) * HD)


def kernel(
    X, Z, Y,
    seg_len, order, q_in, k_in, v_in, w_hbm, gp_in,
    proj_out, dq_out, dk_out, dv_out, gw_out,
    qb, db, kvb, gpf, gpx, segk, segq, pbuf, dpbuf, mst, lst, dst,
    oacc, mrun, st_send, st_recv, sd_send, sd_recv, wbuf, o_send, o_recv, attb, dqacc, dq_send, dq_recv,
    pj_send, pj_recv, fac, delta, part, sib_recv, rs_send, rs_recv,
    gwf, gwp, g_sib, g_send, g_recv,
    w_sem,
    x_ss, x_rs, y_ss, y_rs, ring_ss, ring_rs, ksib_ss, ksib_rs,
    sib_ss, sib_rs, rs_ss, rs_rs, gsib_ss, gsib_rs, g_ss, g_rs,
):
    nplus, nminus = Z // 2, Z - 1 - Z // 2
    QN = X * TOK
    gcols = gp_in.shape[1]
    me = lax.axis_index("ctx")
    y = lax.axis_index("head")
    core = lax.rem(me, 2)
    z = lax.rem(me // 2, Z)
    x = me // (2 * Z)

    def ctx_of(xx, zz, cc):
        return (xx * Z + zz) * 2 + cc

    def zmod(off):
        return lax.rem(z + off + 2 * Z, Z)

    other = 1 - core
    sib = (ctx_of(x, z, other), y)
    up = (ctx_of(x, zmod(1), core), y)
    down = (ctx_of(x, zmod(-1), core), y)

    def x_dev(i):
        return (ctx_of(lax.rem(x + i, X), z, core), y)

    def y_dev(i):
        return (me, lax.rem(y + i, Y))

    def z_dev(i):
        return (ctx_of(x, zmod(i), core), y)

    def rcopy(src, dst_ref, ss, rs, dev):
        return pltpu.make_async_remote_copy(
            src_ref=src, dst_ref=dst_ref, send_sem=ss, recv_sem=rs,
            device_id=dev, device_id_type=MESH,
        )

    barrier = pltpu.get_barrier_semaphore()
    partners = [sib] + [z_dev(i) for i in range(1, Z)]
    partners += [x_dev(i) for i in range(1, X)] + [y_dev(i) for i in range(1, Y)]
    for dev in partners:
        pl.semaphore_signal(barrier, inc=1, device_id=dev, device_id_type=MESH)
    w_copy = pltpu.make_async_copy(w_hbm, wbuf, w_sem)
    w_copy.start()

    sends = []

    def go(copy):
        copy.start()
        sends.append(copy)

    def x_recv(kind, i, buf):
        slot = buf.at[lax.rem(x + X - i, X)]
        rcopy(slot, slot, x_ss.at[kind, i], x_rs.at[kind, i], x_dev(i)).wait_recv()

    def x_send(kind, i, src, buf):
        go(rcopy(src, buf.at[x], x_ss.at[kind, i], x_rs.at[kind, i], x_dev(i)))

    def y_recv(kind, i, buf):
        slot = buf.at[lax.rem(y + Y - i, Y)]
        rcopy(slot, slot, y_ss.at[kind, i], y_rs.at[kind, i], y_dev(i)).wait_recv()

    def y_send(kind, i, src, buf):
        go(rcopy(src, buf.at[y], y_ss.at[kind, i], y_rs.at[kind, i], y_dev(i)))

    half = TOK // 2

    def rows_of(hf):
        return pl.ds(hf * half, half)

    def x_half(kind, i, hf, src_dev):
        slot = db.at[src_dev, rows_of(hf)]
        return rcopy(slot, slot, x_ss.at[kind, i], x_rs.at[kind, i], x_dev(i))

    def y_half(hf, i, src, src_dev):
        slot = gpf.at[src_dev, rows_of(hf)]
        return rcopy(src, slot, y_ss.at[hf, i], y_rs.at[hf, i], y_dev(i))

    def kv_slot(off, cc, a):
        return kvb.at[zmod(off), cc, a]

    def limit(direction, a):
        return nplus if direction == a else nminus

    def ring_send(direction, step, a, src):
        off = 1 - step if direction == 0 else step - 1
        go(rcopy(
            src, kv_slot(off, core, a),
            ring_ss.at[direction, step - 1, a], ring_rs.at[direction, step - 1, a],
            up if direction == 0 else down,
        ))

    def ring_wait(direction, step, a):
        off = -step if direction == 0 else step
        slot = kv_slot(off, core, a)
        rcopy(
            slot, slot, ring_ss.at[direction, step - 1, a],
            ring_rs.at[direction, step - 1, a], up,
        ).wait_recv()

    def sib_index(off):
        return nplus + off if off > 0 else -off

    def ksib_send(off, a, src):
        j = sib_index(off)
        go(rcopy(src, kv_slot(off, core, a), ksib_ss.at[j, a], ksib_rs.at[j, a], sib))

    def ksib_wait(off, a):
        j = sib_index(off)
        slot = kv_slot(off, other, a)
        rcopy(slot, slot, ksib_ss.at[j, a], ksib_rs.at[j, a], sib).wait_recv()

    ends = []
    total = seg_len[0]
    for i in range(SEGS - 1):
        ends.append(total)
        total = total + seg_len[i + 1]

    def segments(row_in_block, ctx_id):
        first = order[2 * ctx_id] * BLK
        second = order[2 * ctx_id + 1] * BLK - BLK
        pos = row_in_block + jnp.where(row_in_block < BLK, first, second)
        seg = jnp.zeros_like(pos)
        for end in ends:
            seg = seg + jnp.where(pos >= end, 1, 0)
        return seg

    lanes = lax.broadcasted_iota(jnp.int32, (1, TOK), 1)
    for xx in range(X):
        segq[:, xx * TOK:(xx + 1) * TOK] = segments(lanes, ctx_of(xx, z, core))
    rows = lax.broadcasted_iota(jnp.int32, (TOK, 128), 0)

    def seg_body(zz, carry):
        for cc in range(2):
            segk[zz, cc * TOK:(cc + 1) * TOK, :] = segments(rows, ctx_of(x, zz, cc))
        return carry

    lax.fori_loop(0, Z, seg_body, 0)
    for h in range(HEADS):
        mrun[h] = jnp.full((1, QN), MAX_FLOOR, F32)
        oacc[h] = jnp.zeros((HD, QN), F32)
        dqacc[h] = jnp.zeros((HD, QN), F32)

    qb[x] = q_in[...]
    kvb[z, core, 0] = k_in[...]
    kvb[z, core, 1] = v_in[...]
    gpf[y] = gp_in[...]
    pl.semaphore_wait(barrier, len(partners))

    def send_gp(hf):
        for i in range(1, Y):
            go(y_half(hf, i, gp_in.at[rows_of(hf)], y))

    send_gp(0)
    for a, src in ((0, k_in), (1, v_in)):
        for direction in range(2):
            if limit(direction, a) >= 1:
                ring_send(direction, 1, a, src)
        ksib_send(0, a, src)
    for i in range(1, X):
        x_send(0, i, q_in, qb)
    send_gp(1)

    def keys(zi, a, h):
        return kvb[zi, :, a, :, head_lanes(h)].reshape(2 * TOK, HD)

    def gathered(buf, h):
        return buf[:, :, head_lanes(h)].reshape(QN, HD)

    def fwd(zi):
        def body(h):
            s = dot_nt(keys(zi, 0, h), gathered(qb, h))
            sk = jnp.concatenate([segk[zi]] * X, axis=1)
            s = jnp.where(sk <= segq[...], s, NEG_FILL)
            m = jnp.maximum(jnp.max(s, axis=0, keepdims=True), MAX_FLOOR)
            p = jnp.exp2((s - m) * EXP2_SCALE)
            pbuf[h, zi] = p
            mst[h, zi] = m
            lst[h, zi] = jnp.sum(p, axis=0, keepdims=True)
            pv = dot_tn(keys(zi, 1, h), p.astype(BF16))
            m_old = mrun[h]
            m_new = jnp.maximum(m_old, m)
            mrun[h] = m_new
            oacc[h] = (
                oacc[h] * jnp.exp2((m_old - m_new) * EXP2_SCALE)
                + pv * jnp.exp2((m - m_new) * EXP2_SCALE)
            )

        for h in range(HEADS):
            body(h)

    def dprob(zi):
        def body(h):
            dp = dot_nt(keys(zi, 1, h), gathered(db, h))
            dpbuf[h, zi] = dp
            dst[h, zi] = jnp.sum(dp * pbuf[h, zi], axis=0, keepdims=True)

        for h in range(HEADS):
            body(h)

    def ring_step(step):
        for a in range(2):
            for direction in range(2):
                off = -step if direction == 0 else step
                far = limit(direction, a)
                if step <= far:
                    ring_wait(direction, step, a)
                    if step < far:
                        ring_send(direction, step + 1, a, kv_slot(off, core, a))
                    ksib_send(-step if step == nplus else off, a, kv_slot(off, core, a))

    def step_offsets(step):
        return [0] if step == 0 else ([-step, step] if step <= nminus else [-step])

    def sib_ready(step):
        for off in step_offsets(step):
            for a in range(2):
                ksib_wait(off, a)

    def over(step, fn):
        offs = step_offsets(step)
        if len(offs) == 1:
            fn(zmod(offs[0]))
        else:
            def body(i, carry):
                fn(zmod(step * (2 * i - 1)))
                return carry

            lax.fori_loop(0, 2, body, 0)

    def dout_half(hf):
        acc = None
        for i in range(Y):
            src_y = lax.rem(y + Y - i, Y)
            if i:
                y_half(hf, i, gpf.at[src_y, rows_of(hf)], src_y).wait_recv()
            w_rows = wbuf[pl.ds(pl.multiple_of(src_y * gcols, gcols), gcols), :]
            term = dot_nn(gpf[src_y, rows_of(hf), :], w_rows)
            acc = term if acc is None else acc + term
        db[x, rows_of(hf), :] = acc.astype(BF16)
        for i in range(1, X):
            go(x_half(1 + hf, i, hf, x))

    w_copy.wait()
    ring_step(1)
    for i in range(1, X):
        x_recv(0, i, qb)
    sib_ready(0)
    over(0, fwd)
    dout_half(0)
    ring_step(2)
    sib_ready(1)
    over(1, fwd)
    dout_half(1)
    ring_step(3)
    sib_ready(2)
    over(2, fwd)
    sib_ready(3)
    over(3, fwd)
    ring_step(4)
    for hf in range(2):
        for i in range(1, X):
            x_half(1 + hf, i, hf, lax.rem(x + X - i, X)).wait_recv()
    for step in range(3):
        over(step, dprob)
    sib_ready(4)
    over(4, fwd)

    inverse, part_w = [], []
    for h in range(HEADS):
        m_top = mrun[h]
        w = jnp.exp2((mst[h] - m_top[None]) * EXP2_SCALE)
        l_sum = jnp.maximum(jnp.sum(lst[h] * w, axis=0), 1e-30)
        inv = 1.0 / l_sum
        part_w.append(w)
        inverse.append(inv)
        st_send[h:h + 1, :] = m_top * EXP2_SCALE + jnp.log2(l_sum)
        o_h = (oacc[h] * inv).astype(BF16)
        for xx in range(X):
            o_send[xx, h * HD:(h + 1) * HD, :] = o_h[:, xx * TOK:(xx + 1) * TOK]
    st_send[HEADS:8, :] = jnp.zeros((8 - HEADS, QN), F32)
    for i in range(1, X):
        x_send(4, i, st_send, st_recv)
    for i in range(1, X):
        x_send(5, i, o_send.at[lax.rem(x + i, X)], o_recv)
    for step in range(3, nplus + 1):
        over(step, dprob)
    for h in range(HEADS):
        sd_send[h:h + 1, :] = jnp.sum(dst[h] * part_w[h], axis=0) * inverse[h]
    sd_send[HEADS:8, :] = jnp.zeros((8 - HEADS, QN), F32)
    for i in range(1, X):
        x_send(6, i, sd_send, sd_recv)
    for i in range(1, X):
        x_send(3, i, gpf.at[lax.rem(x + i, X)], gpx)
    gpx[x] = gpf[x]
    st_recv[x] = st_send[...]
    o_recv[x] = o_send[x]
    sd_recv[x] = sd_send[...]
    for i in range(1, X):
        x_recv(4, i, st_recv)
    lse_all = st_recv[:, 0:HEADS, :]
    top = jnp.max(lse_all, axis=0)
    lse = top + jnp.log2(jnp.sum(jnp.exp2(lse_all - top[None]), axis=0))
    weight = jnp.exp2(lse_all - lse[None])
    for h in range(HEADS):
        fac[h] = jnp.exp2(mst[h] * EXP2_SCALE - lse[h:h + 1][None])
    for i in range(1, X):
        x_recv(6, i, sd_recv)
    delta_all = jnp.sum(weight * sd_recv[:, 0:HEADS, :], axis=0)
    for h in range(HEADS):
        delta[h] = delta_all[h:h + 1]
    own_stats = st_recv[:, 0:HEADS, pl.ds(pl.multiple_of(x * TOK, TOK), TOK)]
    own_top = jnp.max(own_stats, axis=0)
    own_w = jnp.exp2(own_stats - own_top[None])
    own_w = own_w / jnp.sum(own_w, axis=0)[None]

    def dest_off(o):
        pair = o // 2
        return jnp.where(lax.rem(o, 2) == 0, nplus - pair, pair - nminus)

    def bwd(o):
        zi = zmod(dest_off(o))

        def body(h):
            lanes_h = head_lanes(h)
            p = pbuf[h, zi] * fac[h, zi]
            ds = (p * (dpbuf[h, zi] - delta[h])).astype(BF16)
            dv = dot_nn(p.astype(BF16), gathered(db, h)).astype(BF16)
            dk = (dot_nn(ds, gathered(qb, h)) * SCALE).astype(BF16)
            for cc in range(2):
                part[o, cc, 0, :, lanes_h] = dk[cc * TOK:(cc + 1) * TOK]
                part[o, cc, 1, :, lanes_h] = dv[cc * TOK:(cc + 1) * TOK]
            dqacc[h] = dqacc[h] + dot_tn(keys(zi, 0, h), ds)

        for h in range(HEADS):
            body(h)

    def sib_copy(o, a):
        return rcopy(
            part.at[o, other, a], sib_recv.at[o, a], sib_ss.at[o, a], sib_rs.at[o, a], sib
        )

    def rs_copy(o, a):
        if a == 0:
            slot = o + 2
            off = jnp.where(lax.rem(o, 2) == 0, 1, -1)
        else:
            slot = jnp.where(o == 0, 1, o + 2)
            off = jnp.where((lax.rem(o, 2) == 0) & (o > 0), 1, -1)
        return rcopy(
            rs_send.at[o, a], rs_recv.at[slot, a], rs_ss.at[o, a], rs_rs.at[slot, a], z_dev(off)
        )

    def rs_wait(o, a):
        slot = rs_recv.at[o, a]
        rcopy(slot, slot, rs_ss.at[0, a], rs_rs.at[o, a], up).wait_recv()

    def finalize(o, a):
        sib_copy(o, a).wait_recv()
        total = part[o, core, a].astype(F32) + sib_recv[o, a].astype(F32)
        if o >= 2 + a or (a == 1 and o == 1):
            rs_wait(o, a)
            total = total + rs_recv[o, a].astype(F32)
        rs_send[o, a] = total.astype(BF16)
        rs_copy(o, a).start()

    def bwd_range(first, last):
        def body(o, carry):
            bwd(o)
            for a in range(2):
                sib_copy(o, a).start()
            return carry

        lax.fori_loop(first, last, body, 0)

    bwd_range(0, 2)
    finalize(0, 0)
    finalize(0, 1)
    finalize(1, 0)

    for i in range(1, X):
        x_recv(5, i, o_recv)
    for h in range(HEADS):
        o_t = jnp.zeros((HD, TOK), F32)
        for xx in range(X):
            o_t = o_t + o_recv[xx, h * HD:(h + 1) * HD, :].astype(F32) * own_w[xx, h:h + 1]
        attb[x, :, h * HD:(h + 1) * HD] = o_t.T.astype(BF16)
    for i in range(1, X):
        x_send(7, i, attb.at[x], attb)
    bwd_range(2, 5)
    finalize(2, 1)
    finalize(1, 1)
    finalize(2, 0)
    bwd_range(5, Z)

    for h in range(HEADS):
        dq_h = (dqacc[h] * SCALE).astype(BF16)
        for xx in range(X):
            dq_send[xx, h * HD:(h + 1) * HD, :] = dq_h[:, xx * TOK:(xx + 1) * TOK]
    for i in range(1, X):
        x_send(8, i, dq_send.at[lax.rem(x + i, X)], dq_recv)
    dq_recv[x] = dq_send[x]

    att = attb[x]
    for i in range(1, Y):
        dst_y = lax.rem(y + i, Y)
        w_rows = wbuf[pl.ds(pl.multiple_of(dst_y * gcols, gcols), gcols), :]
        pj_send[dst_y] = dot_nt(att, w_rows).astype(BF16)
        y_send(2, i, pj_send.at[dst_y], pj_recv)
    w_rows = wbuf[pl.ds(pl.multiple_of(y * gcols, gcols), gcols), :]
    pj_recv[y] = dot_nt(att, w_rows).astype(BF16)
    for o in (3, 4):
        for a in range(2):
            finalize(o, a)

    for i in range(1, X):
        x_recv(3, i, gpx)
    for i in range(1, X):
        x_recv(7, i, attb)
    att_all = attb[...].reshape(QN, WID)

    def gw_body(j, carry):
        lanes_j = pl.ds(pl.multiple_of(j * 128, 128), 128)
        left = gpx[:, :, lanes_j].reshape(QN, 128)
        gwf[pl.ds(pl.multiple_of(j * 128, 128), 128), :] = dot_tn(left, att_all)
        return carry

    lax.fori_loop(0, gcols // 128, gw_body, 0)
    grow = gw_out.shape[0]
    for zz in range(Z):
        for cc in range(2):
            first = (zz * 2 + cc) * grow
            gwp[cc, zz] = gwf[first:first + grow, :].astype(BF16)
    gsib = rcopy(gwp.at[other], g_sib, gsib_ss, gsib_rs, sib)
    go(gsib)

    for a in range(2):
        finalize(5, a)
    gsib.wait_recv()
    for i in range(1, Z):
        zi = zmod(i)
        g_send[i] = (gwp[core, zi].astype(F32) + g_sib[zi].astype(F32)).astype(BF16)
        go(rcopy(g_send.at[i], g_recv.at[i], g_ss.at[i], g_rs.at[i], z_dev(i)))
    for a in range(2):
        finalize(6, a)

    for i in range(1, Y):
        y_recv(2, i, pj_recv)
    proj = pj_recv[0].astype(F32)
    for yy in range(1, Y):
        proj = proj + pj_recv[yy].astype(F32)
    proj_out[...] = proj.astype(BF16)
    for i in range(1, X):
        x_recv(8, i, dq_recv)
    for h in range(HEADS):
        dq_t = jnp.zeros((HD, TOK), F32)
        for xx in range(X):
            dq_t = dq_t + dq_recv[xx, h * HD:(h + 1) * HD, :].astype(F32)
        dq_out[:, h * HD:(h + 1) * HD] = dq_t.T.astype(BF16)
    g_total = gwp[core, z].astype(F32) + g_sib[z].astype(F32)
    for i in range(1, Z):
        rcopy(g_recv.at[i], g_recv.at[i], g_ss.at[i], g_rs.at[i], z_dev(i)).wait_recv()
        g_total = g_total + g_recv[i].astype(F32)
    gw_out[...] = g_total
    last = Z - 1
    for a, out in ((0, dk_out), (1, dv_out)):
        sib_copy(last, a).wait_recv()
        rs_wait(last, a)
        rs_wait(last + 1, a)
        out[...] = (
            part[last, core, a].astype(F32)
            + sib_recv[last, a].astype(F32)
            + rs_recv[last, a].astype(F32)
            + rs_recv[last + 1, a].astype(F32)
        ).astype(BF16)

    for copy in sends:
        copy.wait_send()
    for a in range(2):
        for o in range(Z):
            sib_copy(o, a).wait_send()
            if o < last:
                rs_copy(o, a).wait_send()


def finish(*refs):
    half = len(refs) // 2
    for src, out in zip(refs[:half], refs[half:]):
        out[...] = src[...]


def per_device(X, Z, Y, queries, key_rows, value_rows, out_weight, grad_projected, segment_len, block_order):
    gcols = grad_projected.shape[1]
    grow = out_weight.shape[0] // (X * Z * 2)
    QN = X * TOK
    vmem = pl.BlockSpec(memory_space=pltpu.VMEM)
    smem = pl.BlockSpec(memory_space=pltpu.SMEM)
    dma = pltpu.SemaphoreType.DMA
    scratch = [
        pltpu.VMEM((X, TOK, WID), BF16),
        pltpu.VMEM((X, TOK, WID), BF16),
        pltpu.VMEM((Z, 2, 2, TOK, WID), BF16),
        pltpu.VMEM((Y, TOK, gcols), BF16),
        pltpu.VMEM((X, TOK, gcols), BF16),
        pltpu.VMEM((Z, 2 * TOK, 128), jnp.int32),
        pltpu.VMEM((1, QN), jnp.int32),
        pltpu.VMEM((HEADS, Z, 2 * TOK, QN), F32),
        pltpu.VMEM((HEADS, Z, 2 * TOK, QN), F32),
        pltpu.VMEM((HEADS, Z, 1, QN), F32),
        pltpu.VMEM((HEADS, Z, 1, QN), F32),
        pltpu.VMEM((HEADS, Z, 1, QN), F32),
        pltpu.VMEM((HEADS, HD, QN), F32),
        pltpu.VMEM((HEADS, 1, QN), F32),
        pltpu.VMEM((8, QN), F32),
        pltpu.VMEM((X, 8, QN), F32),
        pltpu.VMEM((8, QN), F32),
        pltpu.VMEM((X, 8, QN), F32),
        pltpu.VMEM(out_weight.shape, BF16),
        pltpu.VMEM((X, WID, TOK), BF16),
        pltpu.VMEM((X, WID, TOK), BF16),
        pltpu.VMEM((X, TOK, WID), BF16),
        pltpu.VMEM((HEADS, HD, QN), F32),
        pltpu.VMEM((X, WID, TOK), BF16),
        pltpu.VMEM((X, WID, TOK), BF16),
        pltpu.VMEM((Y, TOK, gcols), BF16),
        pltpu.VMEM((Y, TOK, gcols), BF16),
        pltpu.VMEM((HEADS, Z, 1, QN), F32),
        pltpu.VMEM((HEADS, 1, QN), F32),
        pltpu.VMEM((Z, 2, 2, TOK, WID), BF16),
        pltpu.VMEM((Z, 2, TOK, WID), BF16),
        pltpu.VMEM((Z, 2, TOK, WID), BF16),
        pltpu.VMEM((Z + 1, 2, TOK, WID), BF16),
        pltpu.VMEM((gcols, WID), F32),
        pltpu.VMEM((2, Z, grow, WID), BF16),
        pltpu.VMEM((Z, grow, WID), BF16),
        pltpu.VMEM((Z, grow, WID), BF16),
        pltpu.VMEM((Z, grow, WID), BF16),
        dma,
        dma((9, X)), dma((9, X)),
        dma((3, Y)), dma((3, Y)),
        dma((2, Z // 2, 2)), dma((2, Z // 2, 2)),
        dma((Z, 2)), dma((Z, 2)),
        dma((Z, 2)), dma((Z, 2)),
        dma((Z + 1, 2)), dma((Z + 1, 2)),
        dma, dma,
        dma((Z,)), dma((Z,)),
    ]
    out_shape = (
        jax.ShapeDtypeStruct((TOK, gcols), BF16),
        jax.ShapeDtypeStruct((TOK, WID), BF16),
        jax.ShapeDtypeStruct((TOK, WID), BF16),
        jax.ShapeDtypeStruct((TOK, WID), BF16),
        jax.ShapeDtypeStruct((grow, WID), F32),
    )
    results = pl.pallas_call(
        functools.partial(kernel, X, Z, Y),
        out_shape=out_shape,
        in_specs=[smem, smem, vmem, vmem, vmem, pl.BlockSpec(memory_space=pl.ANY), vmem],
        out_specs=(vmem,) * 5,
        scratch_shapes=scratch,
        compiler_params=pltpu.CompilerParams(
            collective_id=0, has_side_effects=True, vmem_limit_bytes=60 * 1024 * 1024
        ),
        name="segment_attention",
    )(segment_len, block_order, queries, key_rows, value_rows, out_weight, grad_projected)
    return pl.pallas_call(
        finish,
        out_shape=out_shape,
        in_specs=[vmem] * 5,
        out_specs=(vmem,) * 5,
        name="outputs",
    )(*results)


def solution(mesh):
    ctx = mesh.shape["ctx"]
    Y = mesh.shape["head"]
    X = Y
    Z = ctx // (2 * X)
    return jax.shard_map(
        functools.partial(per_device, X, Z, Y),
        mesh=mesh,
        in_specs=(
            P("ctx", "head"),
            P("ctx", "head"),
            P("ctx", "head"),
            P(None, "head"),
            P("ctx", "head"),
            P(),
            P(),
        ),
        out_specs=(P("ctx", "head"),) * 5,
        check_vma=False,
    )
```

time: 95.4 us -> 80.8 us (0.85)
  local copies, waits for them, and re-layouts: 7.76 us -> 0 us
  Pallas kernels: 86.8 us -> 80 us
    pallas_call x1, Pallas kernels: 86.8 us -> 78.1 us  [per_device(): pl.pallas_call(functools.partial(kernel, X, Z, Y), out_shape=out_shape, i...]
    unnamed x5 -> x0, local copies, waits for them, and re-layouts: 7.76 us -> none
    pallas_call x0 -> x1, Pallas kernels: none -> 1.93 us  [per_device(): pl.pallas_call(finish, out_shape=out_shape, in_specs=[vmem] * 5, out_spec...]
where the time goes in v2:
time: 80.8 us; the launch traced here: 80.6 us
  Pallas kernels  80 us (99%)
    pallas_call x1, Pallas kernels, per_device(): pl.pallas_call(functools.partial(kernel, X, Z, Y), out_shape=out_shape, i...  78.1 us
    pallas_call x1, Pallas kernels, per_device(): pl.pallas_call(finish, out_shape=out_shape, in_specs=[vmem] * 5, out_spec...  1.93 us

profile of v2, /device:TPU:2, one launch (start us, length us, event | category | flops | bytes accessed | tf_op | source)
XLA Modules:
  0.0 80.6 jit_solution(11067694182949091346)
XLA Ops:
  0.6 78.1 %segment_attention.1 = (bf16[128,768]{1,0:T(8,128)(2,1)}, bf16[128,384]{1,0:T(8,128)(2,1)}, bf16[128,384]{1,0:T(8,128)(2,1)}, bf16[128,384]{1,0:T(8,128)(2,1)}, f32[48,384]{1,0:T(8,128)}) custom-call(s32[8]{0:T(128)} %seg_len.1, s32[128]{0:T(128)} %order.1, bf16[128,384]{1,0:T(8,128)(2,1)} %q_in.1, bf16[128,384]{1,0:T(8,128)(2,1)} %k_in.1, ...), custom_call_target="tpu_custom_call" | custom-call | tf_op jit(solution)/shard_map/segment_attention/pallas_call | solution.py:606
  78.7 1.9 %outputs.1 = (bf16[128,768]{1,0:T(8,128)(2,1)}, bf16[128,384]{1,0:T(8,128)(2,1)}, bf16[128,384]{1,0:T(8,128)(2,1)}, bf16[128,384]{1,0:T(8,128)(2,1)}, f32[48,384]{1,0:T(8,128)}) custom-call(bf16[128,768]{1,0:T(8,128)(2,1)} %get-tuple-element.10.refs_0_, bf16[128,384]{1,0:T(8,128)(2,1)} %get-tuple-element.11.refs_1_, ...), custom_call_target="tpu_custom_call" | custom-call | tf_op jit(solution)/shard_map/outputs/pallas_call | solution.py:617

commit v3 on v2

--- a/solution.py
+++ b/solution.py
@@ -44,11 +44,11 @@
     seg_len, order, q_in, k_in, v_in, w_hbm, gp_in,
     proj_out, dq_out, dk_out, dv_out, gw_out,
     qb, db, kvb, gpf, gpx, segk, segq, pbuf, dpbuf, mst, lst, dst,
-    oacc, mrun, st_send, st_recv, sd_send, sd_recv, wbuf, o_send, o_recv, attb, dqacc, dq_send, dq_recv,
+    oacc, mrun, st_send, st_recv, wbuf, o_send, o_recv, attb, dqacc, dq_send, dq_recv,
     pj_send, pj_recv, fac, delta, part, sib_recv, rs_send, rs_recv,
     gwf, gwp, g_sib, g_send, g_recv,
     w_sem,
-    x_ss, x_rs, y_ss, y_rs, ring_ss, ring_rs, ksib_ss, ksib_rs,
+    x_ss, x_rs, gx_ss, gx_rs, y_ss, y_rs, ring_ss, ring_rs, ksib_ss, ksib_rs,
     sib_ss, sib_rs, rs_ss, rs_rs, gsib_ss, gsib_rs, g_ss, g_rs,
 ):
     nplus, nminus = Z // 2, Z - 1 - Z // 2
@@ -87,7 +87,7 @@
         )
 
     barrier = pltpu.get_barrier_semaphore()
-    partners = [sib] + [z_dev(i) for i in range(1, Z)]
+    partners = [sib] + [z_dev(i) for i in (1, -1, 2, -2)]
     partners += [x_dev(i) for i in range(1, X)] + [y_dev(i) for i in range(1, Y)]
     for dev in partners:
         pl.semaphore_signal(barrier, inc=1, device_id=dev, device_id_type=MESH)
@@ -122,6 +122,22 @@
     def x_half(kind, i, hf, src_dev):
         slot = db.at[src_dev, rows_of(hf)]
         return rcopy(slot, slot, x_ss.at[kind, i], x_rs.at[kind, i], x_dev(i))
+
+    def gx_half(i, hf, src, src_dev):
+        slot = gpx.at[src_dev, rows_of(hf)]
+        src = slot if src is None else src
+        return rcopy(src, slot, gx_ss.at[i, hf], gx_rs.at[i, hf], x_dev(i))
+
+    def o_piece(i, h, src_dev, dst_dev):
+        rows_h = pl.ds(h * HD, HD)
+        return rcopy(
+            o_send.at[dst_dev, rows_h], o_recv.at[src_dev, rows_h],
+            x_ss.at[5 + h, i], x_rs.at[5 + h, i], x_dev(i),
+        )
+
+    def att_piece(i, h, src_dev):
+        slot = attb.at[src_dev, h]
+        return rcopy(slot, slot, x_ss.at[8 + h, i], x_rs.at[8 + h, i], x_dev(i))
 
     def y_half(hf, i, src, src_dev):
         slot = gpf.at[src_dev, rows_of(hf)]
@@ -203,11 +219,12 @@
             go(y_half(hf, i, gp_in.at[rows_of(hf)], y))
 
     send_gp(0)
-    for a, src in ((0, k_in), (1, v_in)):
+    for turn in range(2):
         for direction in range(2):
-            if limit(direction, a) >= 1:
-                ring_send(direction, 1, a, src)
-        ksib_send(0, a, src)
+            a = (direction + turn) % 2
+            ring_send(direction, 1, a, (k_in, v_in)[a])
+    for a in range(2):
+        ksib_send(0, a, (k_in, v_in)[a])
     for i in range(1, X):
         x_send(0, i, q_in, qb)
     send_gp(1)
@@ -250,8 +267,9 @@
             body(h)
 
     def ring_step(step):
-        for a in range(2):
+        for turn in range(2):
             for direction in range(2):
+                a = (direction + turn) % 2
                 off = -step if direction == 0 else step
                 far = limit(direction, a)
                 if step <= far:
@@ -291,6 +309,9 @@
         db[x, rows_of(hf), :] = acc.astype(BF16)
         for i in range(1, X):
             go(x_half(1 + hf, i, hf, x))
+        for i in range(1, X):
+            go(gx_half(i, hf, gpf.at[lax.rem(x + i, X), rows_of(hf)], x))
+        gpx[x, rows_of(hf), :] = gpf[x, rows_of(hf), :]
 
     w_copy.wait()
     ring_step(1)
@@ -308,63 +329,49 @@
     over(2, fwd)
     sib_ready(3)
     over(3, fwd)
+    for hf in range(2):
+        for i in range(1, X):
+            x_half(1 + hf, i, hf, lax.rem(x + X - i, X)).wait_recv()
+    for step in range(2):
+        over(step, dprob)
     ring_step(4)
-    for hf in range(2):
-        for i in range(1, X):
-            x_half(1 + hf, i, hf, lax.rem(x + X - i, X)).wait_recv()
-    for step in range(3):
+    for step in range(2, 4):
         over(step, dprob)
     sib_ready(4)
     over(4, fwd)
-
-    inverse, part_w = [], []
+    over(4, dprob)
+
+    inverse = []
     for h in range(HEADS):
         m_top = mrun[h]
         w = jnp.exp2((mst[h] - m_top[None]) * EXP2_SCALE)
         l_sum = jnp.maximum(jnp.sum(lst[h] * w, axis=0), 1e-30)
         inv = 1.0 / l_sum
-        part_w.append(w)
         inverse.append(inv)
         st_send[h:h + 1, :] = m_top * EXP2_SCALE + jnp.log2(l_sum)
-        o_h = (oacc[h] * inv).astype(BF16)
+        st_send[HEADS + h:HEADS + h + 1, :] = jnp.sum(dst[h] * w, axis=0) * inv
+    st_send[2 * HEADS:8, :] = jnp.zeros((8 - 2 * HEADS, QN), F32)
+    for i in range(1, X):
+        x_send(3, i, st_send, st_recv)
+    for h in range(HEADS):
+        o_h = (oacc[h] * inverse[h]).astype(BF16)
         for xx in range(X):
             o_send[xx, h * HD:(h + 1) * HD, :] = o_h[:, xx * TOK:(xx + 1) * TOK]
-    st_send[HEADS:8, :] = jnp.zeros((8 - HEADS, QN), F32)
-    for i in range(1, X):
-        x_send(4, i, st_send, st_recv)
-    for i in range(1, X):
-        x_send(5, i, o_send.at[lax.rem(x + i, X)], o_recv)
-    for step in range(3, nplus + 1):
-        over(step, dprob)
-    for h in range(HEADS):
-        sd_send[h:h + 1, :] = jnp.sum(dst[h] * part_w[h], axis=0) * inverse[h]
-    sd_send[HEADS:8, :] = jnp.zeros((8 - HEADS, QN), F32)
-    for i in range(1, X):
-        x_send(6, i, sd_send, sd_recv)
-    for i in range(1, X):
-        x_send(3, i, gpf.at[lax.rem(x + i, X)], gpx)
-    gpx[x] = gpf[x]
+        for i in range(1, X):
+            go(o_piece(i, h, x, lax.rem(x + i, X)))
     st_recv[x] = st_send[...]
     o_recv[x] = o_send[x]
-    sd_recv[x] = sd_send[...]
     for i in range(1, X):
-        x_recv(4, i, st_recv)
+        x_recv(3, i, st_recv)
     lse_all = st_recv[:, 0:HEADS, :]
     top = jnp.max(lse_all, axis=0)
     lse = top + jnp.log2(jnp.sum(jnp.exp2(lse_all - top[None]), axis=0))
     weight = jnp.exp2(lse_all - lse[None])
     for h in range(HEADS):
         fac[h] = jnp.exp2(mst[h] * EXP2_SCALE - lse[h:h + 1][None])
-    for i in range(1, X):
-        x_recv(6, i, sd_recv)
-    delta_all = jnp.sum(weight * sd_recv[:, 0:HEADS, :], axis=0)
+    delta_all = jnp.sum(weight * st_recv[:, HEADS:2 * HEADS, :], axis=0)
     for h in range(HEADS):
         delta[h] = delta_all[h:h + 1]
-    own_stats = st_recv[:, 0:HEADS, pl.ds(pl.multiple_of(x * TOK, TOK), TOK)]
-    own_top = jnp.max(own_stats, axis=0)
-    own_w = jnp.exp2(own_stats - own_top[None])
-    own_w = own_w / jnp.sum(own_w, axis=0)[None]
-
     def dest_off(o):
         pair = o // 2
         return jnp.where(lax.rem(o, 2) == 0, nplus - pair, pair - nminus)
@@ -424,35 +431,49 @@
 
         lax.fori_loop(first, last, body, 0)
 
+    turns = (
+        ((0, 0), (0, 1)), ((1, 0), (2, 1)), ((1, 1), (2, 0)), ((3, 0), (4, 1)),
+        ((3, 1), (4, 0)), ((5, 0), (6, 1)), ((5, 1), (6, 0)),
+    )
+
+    def turn_out(n):
+        for o, a in turns[n]:
+            finalize(o, a)
+
     bwd_range(0, 2)
-    finalize(0, 0)
-    finalize(0, 1)
-    finalize(1, 0)
-
-    for i in range(1, X):
-        x_recv(5, i, o_recv)
+    turn_out(0)
+    bwd_range(2, 4)
+    turn_out(1)
+
+    own_stats = st_recv[:, 0:HEADS, pl.ds(pl.multiple_of(x * TOK, TOK), TOK)]
+    own_top = jnp.max(own_stats, axis=0)
+    own_w = jnp.exp2(own_stats - own_top[None])
+    own_w = own_w / jnp.sum(own_w, axis=0)[None]
+
     for h in range(HEADS):
         o_t = jnp.zeros((HD, TOK), F32)
+        for i in range(1, X):
+            o_piece(i, h, lax.rem(x + X - i, X), 0).wait_recv()
         for xx in range(X):
             o_t = o_t + o_recv[xx, h * HD:(h + 1) * HD, :].astype(F32) * own_w[xx, h:h + 1]
-        attb[x, :, h * HD:(h + 1) * HD] = o_t.T.astype(BF16)
-    for i in range(1, X):
-        x_send(7, i, attb.at[x], attb)
-    bwd_range(2, 5)
-    finalize(2, 1)
-    finalize(1, 1)
-    finalize(2, 0)
-    bwd_range(5, Z)
+        attb[x, h] = o_t.T.astype(BF16)
+        for i in range(1, X):
+            go(att_piece(i, h, x))
+    bwd_range(4, 7)
+    turn_out(2)
+    bwd_range(7, Z)
 
     for h in range(HEADS):
         dq_h = (dqacc[h] * SCALE).astype(BF16)
         for xx in range(X):
             dq_send[xx, h * HD:(h + 1) * HD, :] = dq_h[:, xx * TOK:(xx + 1) * TOK]
     for i in range(1, X):
-        x_send(8, i, dq_send.at[lax.rem(x + i, X)], dq_recv)
+        x_send(4, i, dq_send.at[lax.rem(x + i, X)], dq_recv)
     dq_recv[x] = dq_send[x]
 
-    att = attb[x]
+    turn_out(3)
+
+    att = jnp.concatenate([attb[x, h] for h in range(HEADS)], axis=1)
     for i in range(1, Y):
         dst_y = lax.rem(y + i, Y)
         w_rows = wbuf[pl.ds(pl.multiple_of(dst_y * gcols, gcols), gcols), :]
@@ -460,15 +481,17 @@
         y_send(2, i, pj_send.at[dst_y], pj_recv)
     w_rows = wbuf[pl.ds(pl.multiple_of(y * gcols, gcols), gcols), :]
     pj_recv[y] = dot_nt(att, w_rows).astype(BF16)
-    for o in (3, 4):
-        for a in range(2):
-            finalize(o, a)
-
-    for i in range(1, X):
-        x_recv(3, i, gpx)
-    for i in range(1, X):
-        x_recv(7, i, attb)
-    att_all = attb[...].reshape(QN, WID)
+    turn_out(4)
+
+    for hf in range(2):
+        for i in range(1, X):
+            gx_half(i, hf, None, lax.rem(x + X - i, X)).wait_recv()
+    for h in range(HEADS):
+        for i in range(1, X):
+            att_piece(i, h, lax.rem(x + X - i, X)).wait_recv()
+    att_all = jnp.concatenate(
+        [attb[:, h].reshape(QN, HD) for h in range(HEADS)], axis=1
+    )
 
     def gw_body(j, carry):
         lanes_j = pl.ds(pl.multiple_of(j * 128, 128), 128)
@@ -485,15 +508,28 @@
     gsib = rcopy(gwp.at[other], g_sib, gsib_ss, gsib_rs, sib)
     go(gsib)
 
-    for a in range(2):
-        finalize(5, a)
+    turn_out(5)
+
+    def g_copy(idx, off):
+        return rcopy(g_send.at[idx], g_recv.at[idx], g_ss.at[idx], g_rs.at[idx], z_dev(off))
+
+    def g_term(off):
+        zi = zmod(off)
+        return gwp[core, zi].astype(F32) + g_sib[zi].astype(F32)
+
+    def g_get(idx):
+        g_copy(idx, 1).wait_recv()
+        return g_recv[idx].astype(F32)
+
     gsib.wait_recv()
-    for i in range(1, Z):
-        zi = zmod(i)
-        g_send[i] = (gwp[core, zi].astype(F32) + g_sib[zi].astype(F32)).astype(BF16)
-        go(rcopy(g_send.at[i], g_recv.at[i], g_ss.at[i], g_rs.at[i], z_dev(i)))
-    for a in range(2):
-        finalize(6, a)
+    for idx, off, to in ((0, 4, 2), (1, 3, 1), (2, -3, -1), (3, 1, 1), (4, -1, -1)):
+        g_send[idx] = g_term(off).astype(BF16)
+        go(g_copy(idx, to))
+    turn_out(6)
+    g_send[5] = (g_term(2) + g_get(0) + g_get(1)).astype(BF16)
+    go(g_copy(5, 2))
+    g_send[6] = (g_term(-2) + g_get(2)).astype(BF16)
+    go(g_copy(6, -2))
 
     for i in range(1, Y):
         y_recv(2, i, pj_recv)
@@ -502,17 +538,13 @@
         proj = proj + pj_recv[yy].astype(F32)
     proj_out[...] = proj.astype(BF16)
     for i in range(1, X):
-        x_recv(8, i, dq_recv)
+        x_recv(4, i, dq_recv)
     for h in range(HEADS):
         dq_t = jnp.zeros((HD, TOK), F32)
         for xx in range(X):
             dq_t = dq_t + dq_recv[xx, h * HD:(h + 1) * HD, :].astype(F32)
         dq_out[:, h * HD:(h + 1) * HD] = dq_t.T.astype(BF16)
-    g_total = gwp[core, z].astype(F32) + g_sib[z].astype(F32)
-    for i in range(1, Z):
-        rcopy(g_recv.at[i], g_recv.at[i], g_ss.at[i], g_rs.at[i], z_dev(i)).wait_recv()
-        g_total = g_total + g_recv[i].astype(F32)
-    gw_out[...] = g_total
+    gw_out[...] = g_term(0) + g_get(3) + g_get(4) + g_get(5) + g_get(6)
     last = Z - 1
     for a, out in ((0, dk_out), (1, dv_out)):
         sib_copy(last, a).wait_recv()
@@ -564,12 +596,10 @@
         pltpu.VMEM((HEADS, 1, QN), F32),
         pltpu.VMEM((8, QN), F32),
         pltpu.VMEM((X, 8, QN), F32),
-        pltpu.VMEM((8, QN), F32),
-        pltpu.VMEM((X, 8, QN), F32),
         pltpu.VMEM(out_weight.shape, BF16),
         pltpu.VMEM((X, WID, TOK), BF16),
         pltpu.VMEM((X, WID, TOK), BF16),
-        pltpu.VMEM((X, TOK, WID), BF16),
+        pltpu.VMEM((X, HEADS, TOK, HD), BF16),
         pltpu.VMEM((HEADS, HD, QN), F32),
         pltpu.VMEM((X, WID, TOK), BF16),
         pltpu.VMEM((X, WID, TOK), BF16),
@@ -587,7 +617,8 @@
         pltpu.VMEM((Z, grow, WID), BF16),
         pltpu.VMEM((Z, grow, WID), BF16),
         dma,
-        dma((9, X)), dma((9, X)),
+        dma((11, X)), dma((11, X)),
+        dma((X, 2)), dma((X, 2)),
         dma((3, Y)), dma((3, Y)),
         dma((2, Z // 2, 2)), dma((2, Z // 2, 2)),
         dma((Z, 2)), dma((Z, 2)),

time: 80.8 us -> 70.5 us (0.87); the launches traced: 80.6 us -> 69.2 us
  Pallas kernels: 80 us -> 68.6 us
    pallas_call x1, Pallas kernels: 78.1 us -> 66.6 us  [per_device(): pl.pallas_call(functools.partial(kernel, X, Z, Y), out_shape=out_shape, i...]
where the time goes in v3:
time: 70.5 us; the launch traced here: 69.2 us
  Pallas kernels  68.6 us (97%)
    pallas_call x1, Pallas kernels, per_device(): pl.pallas_call(functools.partial(kernel, X, Z, Y), out_shape=out_shape, i...  66.6 us
    pallas_call x1, Pallas kernels, per_device(): pl.pallas_call(finish, out_shape=out_shape, in_specs=[vmem] * 5, out_spec...  1.93 us

profile of v3, /device:TPU:2, one launch (start us, length us, event | category | flops | bytes accessed | tf_op | source)
XLA Modules:
  0.0 69.2 jit_solution(3541690155018615046)
XLA Ops:
  0.6 66.6 %segment_attention.1 = (bf16[128,768]{1,0:T(8,128)(2,1)}, bf16[128,384]{1,0:T(8,128)(2,1)}, bf16[128,384]{1,0:T(8,128)(2,1)}, bf16[128,384]{1,0:T(8,128)(2,1)}, f32[48,384]{1,0:T(8,128)}) custom-call(s32[8]{0:T(128)} %seg_len.1, s32[128]{0:T(128)} %order.1, bf16[128,384]{1,0:T(8,128)(2,1)} %q_in.1, bf16[128,384]{1,0:T(8,128)(2,1)} %k_in.1, ...), custom_call_target="tpu_custom_call" | custom-call | tf_op jit(solution)/shard_map/segment_attention/pallas_call | solution.py:637
  67.3 1.9 %outputs.1 = (bf16[128,768]{1,0:T(8,128)(2,1)}, bf16[128,384]{1,0:T(8,128)(2,1)}, bf16[128,384]{1,0:T(8,128)(2,1)}, bf16[128,384]{1,0:T(8,128)(2,1)}, f32[48,384]{1,0:T(8,128)}) custom-call(bf16[128,768]{1,0:T(8,128)(2,1)} %get-tuple-element.10.refs_0_, bf16[128,384]{1,0:T(8,128)(2,1)} %get-tuple-element.11.refs_1_, ...), custom_call_target="tpu_custom_call" | custom-call | tf_op jit(solution)/shard_map/outputs/pallas_call | solution.py:648

commit v4 on v3

--- a/solution.py
+++ b/solution.py
@@ -41,7 +41,7 @@
 
 def kernel(
     X, Z, Y,
-    seg_len, order, q_in, k_in, v_in, w_hbm, gp_in,
+    seg_len, order, q_hbm, k_hbm, v_hbm, w_hbm, gp_hbm,
     proj_out, dq_out, dk_out, dv_out, gw_out,
     qb, db, kvb, gpf, gpx, segk, segq, pbuf, dpbuf, mst, lst, dst,
     oacc, mrun, st_send, st_recv, wbuf, o_send, o_recv, attb, dqacc, dq_send, dq_recv,
@@ -53,7 +53,7 @@
 ):
     nplus, nminus = Z // 2, Z - 1 - Z // 2
     QN = X * TOK
-    gcols = gp_in.shape[1]
+    gcols = gp_hbm.shape[1]
     me = lax.axis_index("ctx")
     y = lax.axis_index("head")
     core = lax.rem(me, 2)
@@ -91,8 +91,15 @@
     partners += [x_dev(i) for i in range(1, X)] + [y_dev(i) for i in range(1, Y)]
     for dev in partners:
         pl.semaphore_signal(barrier, inc=1, device_id=dev, device_id_type=MESH)
-    w_copy = pltpu.make_async_copy(w_hbm, wbuf, w_sem)
-    w_copy.start()
+    local = [
+        pltpu.make_async_copy(src, dst_ref, w_sem.at[i])
+        for i, (src, dst_ref) in enumerate((
+            (gp_hbm, gpf.at[y]), (k_hbm, kvb.at[z, core, 0]), (v_hbm, kvb.at[z, core, 1]),
+            (q_hbm, qb.at[x]), (w_hbm, wbuf),
+        ))
+    ]
+    for copy in local:
+        copy.start()
 
     sends = []
 
@@ -208,25 +215,23 @@
         oacc[h] = jnp.zeros((HD, QN), F32)
         dqacc[h] = jnp.zeros((HD, QN), F32)
 
-    qb[x] = q_in[...]
-    kvb[z, core, 0] = k_in[...]
-    kvb[z, core, 1] = v_in[...]
-    gpf[y] = gp_in[...]
+    for copy in local[:-1]:
+        copy.wait()
     pl.semaphore_wait(barrier, len(partners))
 
     def send_gp(hf):
         for i in range(1, Y):
-            go(y_half(hf, i, gp_in.at[rows_of(hf)], y))
+            go(y_half(hf, i, gpf.at[y, rows_of(hf)], y))
 
     send_gp(0)
     for turn in range(2):
         for direction in range(2):
             a = (direction + turn) % 2
-            ring_send(direction, 1, a, (k_in, v_in)[a])
+            ring_send(direction, 1, a, kvb.at[z, core, a])
     for a in range(2):
-        ksib_send(0, a, (k_in, v_in)[a])
+        ksib_send(0, a, kvb.at[z, core, a])
     for i in range(1, X):
-        x_send(0, i, q_in, qb)
+        x_send(0, i, qb.at[x], qb)
     send_gp(1)
 
     def keys(zi, a, h):
@@ -266,36 +271,28 @@
         for h in range(HEADS):
             body(h)
 
-    def ring_step(step):
-        for turn in range(2):
-            for direction in range(2):
-                a = (direction + turn) % 2
-                off = -step if direction == 0 else step
-                far = limit(direction, a)
-                if step <= far:
-                    ring_wait(direction, step, a)
-                    if step < far:
-                        ring_send(direction, step + 1, a, kv_slot(off, core, a))
-                    ksib_send(-step if step == nplus else off, a, kv_slot(off, core, a))
-
-    def step_offsets(step):
-        return [0] if step == 0 else ([-step, step] if step <= nminus else [-step])
-
-    def sib_ready(step):
-        for off in step_offsets(step):
-            for a in range(2):
-                ksib_wait(off, a)
-
-    def over(step, fn):
-        offs = step_offsets(step)
-        if len(offs) == 1:
-            fn(zmod(offs[0]))
-        else:
-            def body(i, carry):
-                fn(zmod(step * (2 * i - 1)))
-                return carry
-
-            lax.fori_loop(0, 2, body, 0)
+    def ring_turn(step, turn):
+        for direction in range(2):
+            a = (direction + turn) % 2
+            off = -step if direction == 0 else step
+            far = limit(direction, a)
+            if step <= far:
+                ring_wait(direction, step, a)
+                if step < far:
+                    ring_send(direction, step + 1, a, kv_slot(off, core, a))
+                ksib_send(-step if step == nplus else off, a, kv_slot(off, core, a))
+
+    def fwd_at(off):
+        for a in range(2):
+            ksib_wait(off, a)
+        fwd(zmod(off))
+
+    def dprob_range(first, last):
+        def body(i, carry):
+            dprob(zmod(i))
+            return carry
+
+        lax.fori_loop(first, last, body, 0)
 
     def dout_half(hf):
         acc = None
@@ -309,37 +306,38 @@
         db[x, rows_of(hf), :] = acc.astype(BF16)
         for i in range(1, X):
             go(x_half(1 + hf, i, hf, x))
-        for i in range(1, X):
-            go(gx_half(i, hf, gpf.at[lax.rem(x + i, X), rows_of(hf)], x))
-        gpx[x, rows_of(hf), :] = gpf[x, rows_of(hf), :]
-
-    w_copy.wait()
-    ring_step(1)
+
+    def send_gx():
+        for hf in range(2):
+            for i in range(1, X):
+                go(gx_half(i, hf, gpf.at[lax.rem(x + i, X), rows_of(hf)], x))
+        gpx[x] = gpf[x]
+
+    local[-1].wait()
+    ring_turn(1, 0)
+    ring_turn(1, 1)
+    dout_half(0)
     for i in range(1, X):
         x_recv(0, i, qb)
-    sib_ready(0)
-    over(0, fwd)
-    dout_half(0)
-    ring_step(2)
-    sib_ready(1)
-    over(1, fwd)
+    fwd_at(0)
+    ring_turn(2, 0)
     dout_half(1)
-    ring_step(3)
-    sib_ready(2)
-    over(2, fwd)
-    sib_ready(3)
-    over(3, fwd)
+    ring_turn(2, 1)
+    send_gx()
+    fwd_at(-1)
+    fwd_at(1)
+    ring_turn(3, 0)
+    fwd_at(-2)
+    ring_turn(3, 1)
+    fwd_at(2)
+    fwd_at(-3)
+    ring_turn(4, 0)
+    fwd_at(3)
+    fwd_at(-4)
     for hf in range(2):
         for i in range(1, X):
             x_half(1 + hf, i, hf, lax.rem(x + X - i, X)).wait_recv()
-    for step in range(2):
-        over(step, dprob)
-    ring_step(4)
-    for step in range(2, 4):
-        over(step, dprob)
-    sib_ready(4)
-    over(4, fwd)
-    over(4, dprob)
+    dprob_range(0, Z)
 
     inverse = []
     for h in range(HEADS):
@@ -616,7 +614,7 @@
         pltpu.VMEM((Z, grow, WID), BF16),
         pltpu.VMEM((Z, grow, WID), BF16),
         pltpu.VMEM((Z, grow, WID), BF16),
-        dma,
+        dma((5,)),
         dma((11, X)), dma((11, X)),
         dma((X, 2)), dma((X, 2)),
         dma((3, Y)), dma((3, Y)),
@@ -637,7 +635,7 @@
     results = pl.pallas_call(
         functools.partial(kernel, X, Z, Y),
         out_shape=out_shape,
-        in_specs=[smem, smem, vmem, vmem, vmem, pl.BlockSpec(memory_space=pl.ANY), vmem],
+        in_specs=[smem, smem] + [pl.BlockSpec(memory_space=pl.ANY)] * 5,
         out_specs=(vmem,) * 5,
         scratch_shapes=scratch,
         compiler_params=pltpu.CompilerParams(

time: 70.5 us -> 68.5 us (0.972)
  Pallas kernels: 68.6 us -> 66.9 us
    pallas_call x1, Pallas kernels: 66.6 us -> 65 us  [per_device(): pl.pallas_call(functools.partial(kernel, X, Z, Y), out_shape=out_shape, i...]
where the time goes in v4:
time: 68.5 us; the launch traced here: 67.6 us
  Pallas kernels  66.9 us (98%)
    pallas_call x1, Pallas kernels, per_device(): pl.pallas_call(functools.partial(kernel, X, Z, Y), out_shape=out_shape, i...  65 us
    pallas_call x1, Pallas kernels, per_device(): pl.pallas_call(finish, out_shape=out_shape, in_specs=[vmem] * 5, out_spec...  1.93 us

profile of v4, /device:TPU:2, one launch (start us, length us, event | category | flops | bytes accessed | tf_op | source)
XLA Modules:
  0.0 67.6 jit_solution(10364915585820458005)
XLA Ops:
  0.6 65.0 %segment_attention.1 = (bf16[128,768]{1,0:T(8,128)(2,1)}, bf16[128,384]{1,0:T(8,128)(2,1)}, bf16[128,384]{1,0:T(8,128)(2,1)}, bf16[128,384]{1,0:T(8,128)(2,1)}, f32[48,384]{1,0:T(8,128)}) custom-call(s32[8]{0:T(128)} %seg_len.1, s32[128]{0:T(128)} %order.1, bf16[128,384]{1,0:T(8,128)(2,1)} %q_hbm.1, bf16[128,384]{1,0:T(8,128)(2,1)} %k_hbm.1, ...), custom_call_target="tpu_custom_call" | custom-call | tf_op jit(solution)/shard_map/segment_attention/pallas_call | solution.py:635
  65.6 1.9 %outputs.1 = (bf16[128,768]{1,0:T(8,128)(2,1)}, bf16[128,384]{1,0:T(8,128)(2,1)}, bf16[128,384]{1,0:T(8,128)(2,1)}, bf16[128,384]{1,0:T(8,128)(2,1)}, f32[48,384]{1,0:T(8,128)}) custom-call(bf16[128,768]{1,0:T(8,128)(2,1)} %get-tuple-element.10.refs_0_, bf16[128,384]{1,0:T(8,128)(2,1)} %get-tuple-element.11.refs_1_, ...), custom_call_target="tpu_custom_call" | custom-call | tf_op jit(solution)/shard_map/outputs/pallas_call | solution.py:646

commit v5 on v4

--- a/solution.py
+++ b/solution.py
@@ -322,22 +322,23 @@
     fwd_at(0)
     ring_turn(2, 0)
     dout_half(1)
+    fwd_at(-1)
     ring_turn(2, 1)
     send_gx()
-    fwd_at(-1)
     fwd_at(1)
+    fwd_at(-2)
     ring_turn(3, 0)
-    fwd_at(-2)
+    fwd_at(2)
     ring_turn(3, 1)
-    fwd_at(2)
     fwd_at(-3)
+    fwd_at(3)
     ring_turn(4, 0)
-    fwd_at(3)
-    fwd_at(-4)
     for hf in range(2):
         for i in range(1, X):
             x_half(1 + hf, i, hf, lax.rem(x + X - i, X)).wait_recv()
-    dprob_range(0, Z)
+    dprob_range(Z - 2, Z + 3)
+    fwd_at(-4)
+    dprob_range(3, 6)
 
     inverse = []
     for h in range(HEADS):

time: 68.5 us -> 68.2 us (level)
  no operation moved by 1% of the time
where the time goes in v5:
time: 68.2 us; the launch traced here: 67.2 us
  Pallas kernels  66.6 us (98%)
    pallas_call x1, Pallas kernels, per_device(): pl.pallas_call(functools.partial(kernel, X, Z, Y), out_shape=out_shape, i...  64.6 us
    pallas_call x1, Pallas kernels, per_device(): pl.pallas_call(finish, out_shape=out_shape, in_specs=[vmem] * 5, out_spec...  1.93 us

profile of v5, /device:TPU:2, one launch (start us, length us, event | category | flops | bytes accessed | tf_op | source)
XLA Modules:
  0.0 67.2 jit_solution(6492923700490195104)
XLA Ops:
  0.6 64.6 %segment_attention.1 = (bf16[128,768]{1,0:T(8,128)(2,1)}, bf16[128,384]{1,0:T(8,128)(2,1)}, bf16[128,384]{1,0:T(8,128)(2,1)}, bf16[128,384]{1,0:T(8,128)(2,1)}, f32[48,384]{1,0:T(8,128)}) custom-call(s32[8]{0:T(128)} %seg_len.1, s32[128]{0:T(128)} %order.1, bf16[128,384]{1,0:T(8,128)(2,1)} %q_hbm.1, bf16[128,384]{1,0:T(8,128)(2,1)} %k_hbm.1, ...), custom_call_target="tpu_custom_call" | custom-call | tf_op jit(solution)/shard_map/segment_attention/pallas_call | solution.py:636
  65.3 1.9 %outputs.1 = (bf16[128,768]{1,0:T(8,128)(2,1)}, bf16[128,384]{1,0:T(8,128)(2,1)}, bf16[128,384]{1,0:T(8,128)(2,1)}, bf16[128,384]{1,0:T(8,128)(2,1)}, f32[48,384]{1,0:T(8,128)}) custom-call(bf16[128,768]{1,0:T(8,128)(2,1)} %get-tuple-element.10.refs_0_, bf16[128,384]{1,0:T(8,128)(2,1)} %get-tuple-element.11.refs_1_, ...), custom_call_target="tpu_custom_call" | custom-call | tf_op jit(solution)/shard_map/outputs/pallas_call | solution.py:647
